TPU v7x, 32 devices: a whole 2x2x4 slice. The times are simulated.
32 devices in a mesh: dp: 8 (over y, x, core), feat: 4 (over z).
Axes of the slice: x: 2, y: 2, z: 4, core: 2. Of those that a mesh axis runs over, the one named last changes fastest.
Arguments:
- tokens: bfloat16 [1024, 8192], P('dp', 'feat'), may hold values from -6 to 6
- targets: bfloat16 [2048, 8192], P('dp', 'feat'), may hold values from -6 to 6
- first_blocks: bfloat16 [128, 64, 256], P('feat'), may hold values from -0.75 to 0.75
- second_factor_blocks: bfloat16 [128, 256, 256], P('feat'), may hold values from -0.375 to 0.375
- down_blocks: bfloat16 [128, 256, 64], P('feat'), may hold values from -0.375 to 0.375
- first_tangent: bfloat16 [128, 64, 256], P('feat'), may hold values from -0.75 to 0.75
- second_factor_tangent: bfloat16 [128, 256, 256], P('feat'), may hold values from -0.375 to 0.375
- doc_lengths: int32 [8, 8], replicated, may hold values from 1 to 32, as said below
- doc_owners: int32 [8, 8], replicated, may hold values from 0 to 7, as said below
- pack_offsets: int32 [8, 8], replicated, may hold values from 0 to 224, as said below
Outputs:
- hess_first: float32 [128, 64, 256], P('feat', 'dp')
- hess_mixed: float32 [128, 256, 256], P('feat', 'dp')
Inputs may be any that keep to these rules, and one draw needn't show every extreme that they name: `doc_lengths`: the 8 lengths of one loader sum to 128; the longest has exactly 32 rows. `doc_owners`: A loader sends exactly one document to each owner; some owner receives exactly 256 rows in all, and none more. `pack_offsets`: each owner's documents lie end to end from row 0 of its pack, in the order of their loaders.
All inputs are finite; a program needn't handle non-finite values.
Results may differ from a plain program's by a relative error of at most 0.0072.
Values may be sent and summed in bfloat16 or wider, within the bound.
A program may use at most 128 MiB of HBM per device.

v0:
```python
import jax
import jax.numpy as jnp
from jax import lax
from jax.sharding import PartitionSpec as P

inv_root_two = 0.7071067811865476
inv_root_two_pi = 0.3989422804014327


def curvature(
    tok_rows,
    goal_rows,
    weight,
    first_blocks,
    second_factor_blocks,
    down_blocks,
    first_tangent,
    second_factor_tangent,
):
    features = lax.axis_size("feat")
    row_count = tok_rows.shape[0]
    local_blocks, block_in, block_out = first_blocks.shape
    pair_size = block_out // (local_blocks * features)
    token_blocks = tok_rows.reshape(row_count, local_blocks, block_in)
    goal_blocks = goal_rows.reshape(row_count, local_blocks, block_in)
    split_shape = (local_blocks, block_in, features, local_blocks, pair_size)
    down_shape = (local_blocks, features, local_blocks, pair_size, block_in)
    first_act = jnp.einsum(
        "rki,kiGgc->Ggkcr",
        token_blocks,
        first_blocks.reshape(split_shape),
        preferred_element_type=jnp.float32,
    ).astype(jnp.bfloat16)
    tangents = jnp.einsum(
        "rki,kiGgc->Ggkcr",
        token_blocks,
        first_tangent.reshape(split_shape),
        preferred_element_type=jnp.float32,
    ).astype(jnp.bfloat16)
    out_grad = (
        jnp.einsum(
            "rkd,kGgcd->Ggkcr",
            goal_blocks,
            down_blocks.reshape(down_shape),
            preferred_element_type=jnp.float32,
        )
        * weight
    ).astype(jnp.bfloat16)
    mixed_activation, mixed_tangent_value, hidden_grad = (
        lax.all_to_all(first_act, "feat", split_axis=0, concat_axis=2, tiled=True),
        lax.all_to_all(tangents, "feat", split_axis=0, concat_axis=2, tiled=True),
        lax.all_to_all(out_grad, "feat", split_axis=0, concat_axis=2, tiled=True),
    )
    hidden_shape = (local_blocks, block_out, row_count)
    mixed_activation = mixed_activation.reshape(hidden_shape)
    mixed_tangent_value = mixed_tangent_value.reshape(hidden_shape)
    hidden_grad = hidden_grad.reshape(hidden_shape)
    pre_act = jnp.einsum(
        "vca,vcf->vfa", mixed_activation, second_factor_blocks, preferred_element_type=jnp.float32
    )
    pre_tan = jnp.einsum(
        "vca,vcf->vfa",
        mixed_tangent_value,
        second_factor_blocks,
        preferred_element_type=jnp.float32,
    ) + jnp.einsum(
        "vca,vcf->vfa", mixed_activation, second_factor_tangent, preferred_element_type=jnp.float32
    )
    density = jnp.exp(-0.5 * pre_act * pre_act) * inv_root_two_pi
    normal_cdf = 0.5 * (1.0 + lax.erf(pre_act * inv_root_two))
    preactivation_gradient = (hidden_grad * (normal_cdf + pre_act * density)).astype(jnp.bfloat16)
    preactivation_tangent_gradient = (
        hidden_grad * (density * (2.0 - pre_act * pre_act)) * pre_tan
    ).astype(jnp.bfloat16)
    hess_mixed = jnp.einsum(
        "evp,eqp->evq",
        mixed_tangent_value,
        preactivation_gradient,
        preferred_element_type=jnp.float32,
    ) + jnp.einsum(
        "evp,eqp->evq",
        mixed_activation,
        preactivation_tangent_gradient,
        preferred_element_type=jnp.float32,
    )
    back_mixed = jnp.einsum(
        "bip,bfi->bfp",
        preactivation_tangent_gradient,
        second_factor_blocks,
        preferred_element_type=jnp.float32,
    ) + jnp.einsum(
        "bip,bfi->bfp",
        preactivation_gradient,
        second_factor_tangent,
        preferred_element_type=jnp.float32,
    )
    back_split = back_mixed.astype(jnp.bfloat16).reshape(
        local_blocks, features, local_blocks, pair_size, row_count
    )
    back_first = lax.all_to_all(back_split, "feat", split_axis=1, concat_axis=0, tiled=True)
    back_first = back_first.reshape(local_blocks * features, local_blocks, pair_size, row_count)
    hess_first = jnp.einsum(
        "gkcr,rki->kigc", back_first, token_blocks, preferred_element_type=jnp.float32
    ).reshape(local_blocks, block_in, block_out)
    return (hess_first, hess_mixed)


def per_device(
    tokens,
    targets,
    first_blocks,
    second_factor_blocks,
    down_blocks,
    first_tangent,
    second_factor_tangent,
    doc_lengths,
    doc_owners,
    pack_offsets,
):
    loaders = lax.axis_size("dp")
    device = lax.axis_index("dp")
    tok_count = tokens.shape[0]
    feature_cols = tokens.shape[1]
    slot_rows = 2 * tok_count // loaders
    my_lengths = lax.dynamic_index_in_dim(doc_lengths, device, 0, keepdims=False)
    my_owners = lax.dynamic_index_in_dim(doc_owners, device, 0, keepdims=False)
    my_starts = jnp.cumsum(my_lengths) - my_lengths
    position = jnp.arange(slot_rows, dtype=jnp.int32)
    owner_ids = jnp.arange(loaders, dtype=jnp.int32)
    matched = (owner_ids[:, None] == my_owners[None, :]).astype(jnp.int32)
    first_row = jnp.sum(matched * my_starts[None, :], axis=1)
    doc_span = jnp.sum(matched * my_lengths[None, :], axis=1)
    in_slot = position[None, :] < doc_span[:, None]
    source = jnp.where(in_slot, first_row[:, None] + position[None, :], 0)
    picked = jnp.take(tokens, source.reshape(-1), axis=0).reshape(loaders, slot_rows, feature_cols)
    outgoing = jnp.where(in_slot[:, :, None], picked, jnp.zeros_like(picked))
    arrived = lax.all_to_all(outgoing, "dp", split_axis=0, concat_axis=0, tiled=True)
    pack_rows = targets.shape[0]
    pack_index = jnp.arange(pack_rows, dtype=jnp.int32)[:, None, None]
    owned = (doc_owners == device)[None, :, :]
    inside = (
        owned
        & (pack_index >= pack_offsets[None, :, :])
        & (pack_index < (pack_offsets + doc_lengths)[None, :, :])
    )
    inside_int = inside.astype(jnp.int32)
    sender = jnp.arange(loaders, dtype=jnp.int32)[None, :, None]
    source_row = jnp.sum(
        inside_int * (sender * slot_rows + pack_index - pack_offsets[None, :, :]), axis=(1, 2)
    )
    filled = jnp.sum(inside_int, axis=(1, 2)) > 0
    weight = jnp.sum(
        inside.astype(jnp.float32) / doc_lengths.astype(jnp.float32)[None, :, :], axis=(1, 2)
    )
    routed = jnp.take(arrived.reshape(loaders * slot_rows, feature_cols), source_row, axis=0)
    routed = jnp.where(filled[:, None], routed, jnp.zeros_like(routed))
    partial_loss_value = curvature(
        routed,
        targets,
        weight,
        first_blocks,
        second_factor_blocks,
        down_blocks,
        first_tangent,
        second_factor_tangent,
    )
    hess_first, hess_mixed = (
        lax.psum_scatter(partial_loss_value[0], "dp", scatter_dimension=1, tiled=True),
        lax.psum_scatter(partial_loss_value[1], "dp", scatter_dimension=1, tiled=True),
    )
    return (hess_first, hess_mixed)


def solution(mesh):
    in_specs = (
        P("dp", "feat"),
        P("dp", "feat"),
        P("feat", None, None),
        P("feat", None, None),
        P("feat", None, None),
        P("feat", None, None),
        P("feat", None, None),
        P(),
        P(),
        P(),
    )
    out_specs = (P("feat", "dp", None), P("feat", "dp", None))
    return jax.shard_map(
        per_device, mesh=mesh, in_specs=in_specs, out_specs=out_specs, check_vma=False
    )
```

profile of v0, /device:TPU:0, one launch (start us, length us, event | category | flops | bytes accessed | tf_op | source)
XLA Modules:
  0.0 619.9 jit_solution(11055322032925525122)
XLA Ops:
  12.5 5.3 all-to-all-start
  19.3 4.7 copy.77
  24.1 3.2 fusion.14
  27.4 2.4 copy.80
  29.8 3.4 all-to-all-done
  33.2 4.9 all-to-all-start.1
  38.1 3.8 copy.86
  44.0 3.5 convert_bitcast_fusion
  50.0 78.9 %all-to-all-done.1 = bf16[4,32,32,2,256]{4,1,3,2,0:T(8,128)(2,1)} async-done(((bf16[4,32,32,2,256]{4,1,3,2,0:T(8,128)(2,1)}), bf16[4,32,32,2,256]{4,1,3,2,0:T(8,128)(2,1)}, u32[]{:S(2)}, u32[]{:S(2)}) %all-to-all-start.1) | async-done | bytes 4194336 | tf_op jit(solution)/shard_map/all_to_all | solution.py:52
  128.9 5.4 all-to-all-start.3
  134.3 3.8 copy.81
  138.1 3.2 convert_bitcast_fusion.1
  143.7 83.2 %all-to-all-done.3 = bf16[4,32,32,2,256]{4,1,3,2,0:T(8,128)(2,1)} async-done(((bf16[4,32,32,2,256]{4,1,3,2,0:T(8,128)(2,1)}), bf16[4,32,32,2,256]{4,1,3,2,0:T(8,128)(2,1)}, u32[]{:S(2)}, u32[]{:S(2)}) %all-to-all-start.3) | async-done | bytes 4194336 | tf_op jit(solution)/shard_map/all_to_all | solution.py:51
  226.9 4.9 all-to-all-start.2
  231.8 6.6 %bitcast_convert_fusion = f32[4,1,32,32,2,256]{5,2,4,3,0,1:T(8,128)} fusion(bf16[4,32,32,2,256]{4,1,3,2,0:T(8,128)(2,1)} %all-to-all-done.1), kind=kLoop, calls=%fused_computation.23 | loop fusion | flops 2097152 | bytes 12582912 | tf_op jit(solution)/shard_map/convert_element_type | solution.py:73
  238.4 9.9 %copy.85 = f32[32,256,256]{1,2,0:T(8,128)} copy(f32[32,256,256]{2,0,1:T(8,128)} %bitcast.92) | data formatting | bytes 16777216 | tf_op jit(solution)/shard_map/convert_element_type | solution.py:73
  248.3 11.8 %fusion.16 = f32[32,256,256]{2,1,0:T(8,128)} fusion(bf16[32,256,256]{2,1,0:T(8,128)(2,1)} %param.13, bf16[32,256,256]{2,0,1:T(8,128)(2,1)} %bitcast.32), kind=kOutput, calls=%fused_computation.26 | convolution fusion | flops 1073741824 | bytes 16777216 | tf_op jit(solution)/shard_map/vca,vcf->vfa/dot_general | solution.py:61
  260.1 64.4 %all-to-all-done.2 = bf16[4,32,32,2,256]{4,1,3,2,0:T(8,128)(2,1)} async-done(((bf16[4,32,32,2,256]{4,1,3,2,0:T(8,128)(2,1)}), bf16[4,32,32,2,256]{4,1,3,2,0:T(8,128)(2,1)}, u32[]{:S(2)}, u32[]{:S(2)}) %all-to-all-start.2) | async-done | bytes 4194336 | tf_op jit(solution)/shard_map/all_to_all | solution.py:50
  324.5 11.8 %fusion.9 = (bf16[32,256,256]{1,2,0:T(8,128)(2,1)}, f32[32,256,256]{2,1,0:T(8,128)}) fusion(f32[32,256,256]{1,2,0:T(8,128)} %copy.85, bf16[32,256,256]{2,1,0:T(8,128)(2,1)} %param.13, bf16[32,256,256]{2,0,1:T(8,128)(2,1)} %bitcast.25), kind=kOutput, calls=%fused_computation.12 | convolution fusion | flops 1094713344 | bytes 29360128 | tf_op jit(solution)/shard_map/vca,vcf->vfa/dot_general | solution.py:58
  336.3 19.5 %fusion.6 = bf16[32,256,256]{1,2,0:T(8,128)(2,1)S(1)} fusion(f32[32,256,256]{1,2,0:T(8,128)} %copy.85, f32[32,256,256]{2,1,0:T(8,128)} %get-tuple-element.17, f32[32,256,256]{2,1,0:T(8,128)} %fusion.16, bf16[32,256,256]{2,1,0:T(8,128)(2,1)S(1)} %copy-done.3, bf16[32,256,256]{2,0,1:T(8,128)(2,1)} %bitcast.25), kind=kOutput, calls=%fused_computation.9 | convolution fusion | flops 1094713344 | bytes 37748736 | tf_op jit(solution)/shard_map/vca,vcf->vfa/dot_general | solution.py:66
  355.8 8.2 %fusion.51 = f32[32,256,256]{1,2,0:T(8,128)} fusion(bf16[32,256,256]{1,2,0:T(8,128)(2,1)S(1)} %fusion.6, bf16[32,256,256]{2,1,0:T(8,128)(2,1)} %param.13), kind=kOutput, calls=%fused_computation.86 | convolution fusion | flops 1073741824 | bytes 16777216 | tf_op jit(solution)/shard_map/bip,bfi->bfp/dot_general | solution.py:86
  364.0 8.0 %fusion.15 = bf16[32,256,256]{2,1,0:T(8,128)(2,1)} fusion(f32[32,256,256]{1,2,0:T(8,128)} %fusion.51, bf16[32,256,256]{1,2,0:T(8,128)(2,1)} %get-tuple-element.16, bf16[32,256,256]{2,1,0:T(8,128)(2,1)S(1)} %copy-done.3), kind=kOutput, calls=%fused_computation.22 | convolution fusion | flops 1077936128 | bytes 20971520 | tf_op jit(solution)/shard_map/bip,bfi->bfp/dot_general | solution.py:91
  372.0 7.4 %reshape.212 = bf16[32,4,32,2,256]{4,3,2,1,0:T(2,128)(2,1)} reshape(bf16[32,256,256]{2,1,0:T(8,128)(2,1)} %fusion.15) | data formatting | bytes 8388608 | tf_op jit(solution)/shard_map/reshape | solution.py:97
  379.4 6.1 copy.94
  385.5 95.4 %all_to_all.59 = bf16[32,4,32,2,256]{4,3,2,0,1:T(2,128)(2,1)S(1)} all-to-all(bf16[32,4,32,2,256]{4,3,2,0,1:T(2,128)(2,1)S(1)} %copy.94), channel_id=1, replica_groups=mesh['dp'=8,'feat'=4] {'feat'}, dimensions={1} | all-to-all | bytes 8388608 | tf_op jit(solution)/shard_map/all_to_all | solution.py:100
  480.9 3.4 copy.95
  485.7 4.5 copy.96
  490.2 5.2 copy.97
  495.7 6.4 %fusion.26 = f32[32,256,256]{2,1,0:T(8,128)S(1)} fusion(bf16[32,256,256]{1,2,0:T(8,128)(2,1)} %copy-done.2, bf16[32,256,256]{2,0,1:T(8,128)(2,1)} %bitcast.25), kind=kOutput, calls=%fused_computation.34 | convolution fusion | flops 1073741824 | bytes 16777216 | tf_op jit(solution)/shard_map/evp,eqp->evq/dot_general | solution.py:80
  502.1 8.9 %fusion.20 = f32[32,256,256]{2,1,0:T(8,128)} fusion(f32[32,256,256]{2,1,0:T(8,128)S(1)} %fusion.26, bf16[32,256,256]{1,2,0:T(8,128)(2,1)S(1)} %copy-done.4, bf16[32,256,256]{2,0,1:T(8,128)(2,1)} %bitcast.32), kind=kOutput, calls=%fused_computation.30 | convolution fusion | flops 1075838976 | bytes 25165824 | tf_op jit(solution)/shard_map/evp,eqp->evq/dot_general | solution.py:75
  511.0 25.8 %reduce-scatter.3.cloned.1.call-done = f32[32,8,256]{2,0,1:T(8,128)} async-done(((f32[32,64,256]{2,0,1:T(8,128)}), f32[32,8,256]{2,0,1:T(8,128)}) %reduce-scatter.3.cloned.1.call-update) | async-done | bytes 262160 | tf_op jit(solution)/shard_map/reduce_scatter | solution.py:168
  538.6 73.9 %reduce-scatter.5.cloned.1.call-done = f32[32,32,256]{2,1,0:T(8,128)} async-done(((f32[32,256,256]{2,1,0:T(8,128)}), f32[32,32,256]{2,1,0:T(8,128)}) %reduce-scatter.5.cloned.1.call-update) | async-done | bytes 1048592 | tf_op jit(solution)/shard_map/reduce_scatter | solution.py:169
  (56 shorter events, 17.4 us)
Async XLA Ops:
  7.2 2.8 copy-start
  12.5 11.5 %copy-start.10 = (s32[8,8]{1,0:T(8,128)S(1)}, s32[8,8]{1,0:T(8,128)}, u32[]{:S(2)}) copy-start(s32[8,8]{1,0:T(8,128)} %param.18) | copy-start | bytes 772
  12.5 11.5 %copy-start.9 = (s32[8,8]{1,0:T(8,128)S(1)}, s32[8,8]{1,0:T(8,128)}, u32[]{:S(2)}) copy-start(s32[8,8]{1,0:T(8,128)} %param.19) | copy-start | bytes 772
  12.5 11.5 %copy-start.11 = (s32[8,8]{1,0:T(8,128)S(1)}, s32[8,8]{1,0:T(8,128)}, u32[]{:S(2)}) copy-start(s32[8,8]{1,0:T(8,128)} %param.17) | copy-start | bytes 772
  12.5 20.7 %all-to-all-start = ((bf16[8,32,2048]{2,1,0:T(8,128)(2,1)}), bf16[8,32,2048]{2,1,0:T(8,128)(2,1)S(1)}, u32[]{:S(2)}, u32[]{:S(2)}) async-start(bf16[8,32,2048]{2,1,0:T(8,128)(2,1)} %select_select_fusion.1), calls=%async_computation | async-start | bytes 2097152 | tf_op jit(solution)/shard_map/all_to_all | solution.py:137
  29.8 8.3 %copy-start.7 = (bf16[32,64,256]{2,1,0:T(8,128)(2,1)S(1)}, bf16[32,64,256]{2,1,0:T(8,128)(2,1)}, u32[]{:S(2)}) copy-start(bf16[32,64,256]{2,1,0:T(8,128)(2,1)} %param.15) | copy-start | bytes 3145732
  33.2 95.7 %all-to-all-start.1 = ((bf16[4,32,32,2,256]{4,1,3,2,0:T(8,128)(2,1)}), bf16[4,32,32,2,256]{4,1,3,2,0:T(8,128)(2,1)}, u32[]{:S(2)}, u32[]{:S(2)}) async-start(bf16[4,32,32,2,256]{4,1,3,2,0:T(8,128)(2,1)} %copy.80), calls=%async_computation.1 | async-start | bytes 8388608 | tf_op jit(solution)/shard_map/all_to_all | solution.py:52
  44.0 94.1 %copy-start.5 = (bf16[256,2048]{0,1:T(8,128)(2,1)}, bf16[256,2048]{0,1:T(8,128)(2,1)S(1)}, u32[]{:S(2)}) copy-start(bf16[256,2048]{0,1:T(8,128)(2,1)S(1)} %copy.76) | copy-start | bytes 3145732
  50.0 84.3 %copy-start.8 = (bf16[32,64,256]{2,1,0:T(8,128)(2,1)S(1)}, bf16[32,64,256]{2,1,0:T(8,128)(2,1)}, u32[]{:S(2)}) copy-start(bf16[32,64,256]{2,1,0:T(8,128)(2,1)} %param.12) | copy-start | bytes 3145732
  128.9 98.0 %all-to-all-start.3 = ((bf16[4,32,32,2,256]{4,1,3,2,0:T(8,128)(2,1)}), bf16[4,32,32,2,256]{4,1,3,2,0:T(8,128)(2,1)}, u32[]{:S(2)}, u32[]{:S(2)}) async-start(bf16[4,32,32,2,256]{4,1,3,2,0:T(8,128)(2,1)} %copy.88), calls=%async_computation.3 | async-start | bytes 8388608 | tf_op jit(solution)/shard_map/all_to_all | solution.py:51
  226.9 97.6 %all-to-all-start.2 = ((bf16[4,32,32,2,256]{4,1,3,2,0:T(8,128)(2,1)}), bf16[4,32,32,2,256]{4,1,3,2,0:T(8,128)(2,1)}, u32[]{:S(2)}, u32[]{:S(2)}) async-start(bf16[4,32,32,2,256]{4,1,3,2,0:T(8,128)(2,1)} %copy.83), calls=%async_computation.2 | async-start | bytes 8388608 | tf_op jit(solution)/shard_map/all_to_all | solution.py:50
  231.8 305.1 %reduce-scatter.3.cloned.1.call-start = ((), (), s32[]{:S(2)}) async-start(), calls=%async_computation.7 | async-start | bytes 2359296 | tf_op jit(solution)/shard_map/reduce_scatter | solution.py:168
  324.5 11.8 %copy-start.3 = (bf16[32,256,256]{2,1,0:T(8,128)(2,1)S(1)}, bf16[32,256,256]{2,1,0:T(8,128)(2,1)}, u32[]{:S(2)}) copy-start(bf16[32,256,256]{2,1,0:T(8,128)(2,1)} %param.16) | copy-start | bytes 12582916
  355.8 8.2 %copy-start.2 = (bf16[32,256,256]{1,2,0:T(8,128)(2,1)}, bf16[32,256,256]{1,2,0:T(8,128)(2,1)S(1)}, u32[]{:S(2)}) copy-start(bf16[32,256,256]{1,2,0:T(8,128)(2,1)S(1)} %fusion.6) | copy-start | bytes 12582916
  480.9 3.4 copy-start.6
  495.4 117.2 %reduce-scatter.5.cloned.1.call-start = ((), (), s32[]{:S(2)}) async-start(), calls=%async_computation.8 | async-start | bytes 9437184 | tf_op jit(solution)/shard_map/reduce_scatter | solution.py:169
  495.7 6.4 %copy-start.4 = (bf16[32,256,256]{1,2,0:T(8,128)(2,1)S(1)}, bf16[32,256,256]{1,2,0:T(8,128)(2,1)}, u32[]{:S(2)}) copy-start(bf16[32,256,256]{1,2,0:T(8,128)(2,1)} %get-tuple-element.16) | copy-start | bytes 12582916
  511.0 101.6 %copy-start.1 = (bf16[128,2048]{1,0:T(8,128)(2,1)S(1)}, bf16[128,2048]{1,0:T(8,128)(2,1)}, u32[]{:S(2)}) copy-start(bf16[128,2048]{1,0:T(8,128)(2,1)} %param.10) | copy-start | bytes 1572868
Sparse Core Ops, SparseCore 0:
  495.5 41.2 reduce-scatter.2
  541.3 71.2 reduce-scatter.4
where the time goes:
time: 628 us; the launch traced here: 620 us
  waiting for transfers between devices  330 us (53%)
  blocking collectives  95.4 us (15%)
  matrix products  85.8 us (14%)
  local copies, waits for them, and re-layouts  64.2 us (10%)
  starting transfers between devices  20.8 us (3%)
  between operations  14.7 us (2%)
  other arithmetic  9.28 us (1%)
    all_to_all x1, blocking collectives, curvature(): lax.all_to_all(back_split, 'feat', split_axis=1, concat_axis=0, tiled=True)  95.4 us
    all_to_all x1, waiting for transfers between devices, curvature(): lax.all_to_all(tangents, 'feat', split_axis=0, concat_axis=2, tiled=True)  83.2 us
    all_to_all x1, waiting for transfers between devices, curvature(): lax.all_to_all(out_grad, 'feat', split_axis=0, concat_axis=2, tiled=True)  78.9 us
    reduce_scatter x1, waiting for transfers between devices, per_device(): lax.psum_scatter(partial_loss_value[1], 'dp', scatter_dimension=1, tiled=...  73.9 us
    all_to_all x1, waiting for transfers between devices, curvature(): lax.all_to_all(first_act, 'feat', split_axis=0, concat_axis=2, tiled=True)  64.4 us
    reduce_scatter x1, waiting for transfers between devices, per_device(): lax.psum_scatter(partial_loss_value[0], 'dp', scatter_dimension=1, tiled=...  25.8 us
    dot_general x1, matrix products, curvature(): jnp.einsum('vca,vcf->vfa', mixed_activation, second_factor_tangent, prefe...  19.5 us
    unnamed x29, local copies, waits for them, and re-layouts  15.7 us
  transfers between devices with their start and end apart: 6, of which 6 were waited for; matrix products, arithmetic and copies ran while one was open for 13% of the time, Pallas kernels for 0%

commit v1 on v0

v1 whole, which is shorter than its diff:
```python
import jax
import jax.numpy as jnp
from jax import lax
from jax.experimental import pallas as pl
from jax.experimental.pallas import tpu as pltpu
from jax.sharding import PartitionSpec as P

inv_root_two = 0.7071067811865476
inv_root_two_pi = 0.3989422804014327
STEP = 2


def mixed_kernel(act_ref, tan_ref, grad_ref, fac_ref, fac_tan_ref, hess_ref, back_ref):
    rows = act_ref.shape[2]
    for b in range(act_ref.shape[0]):
        act = act_ref[b]
        tan = tan_ref[b]
        fac = fac_ref[b]
        fac_tan = fac_tan_ref[b]
        first_dims = (((0,), (0,)), ((), ()))
        both = lax.dot_general(
            fac,
            jnp.concatenate([act, tan], axis=1),
            first_dims,
            preferred_element_type=jnp.float32,
        )
        pre_act = both[:, :rows]
        pre_tan = both[:, rows:] + lax.dot_general(
            fac_tan, act, first_dims, preferred_element_type=jnp.float32
        )
        grad = grad_ref[b].astype(jnp.float32)
        density = jnp.exp(-0.5 * pre_act * pre_act) * inv_root_two_pi
        cdf = 0.5 * (1.0 + lax.erf(pre_act * inv_root_two))
        pre_grad = (grad * (cdf + pre_act * density)).astype(jnp.bfloat16)
        pre_tan_grad = (grad * (density * (2.0 - pre_act * pre_act)) * pre_tan).astype(
            jnp.bfloat16
        )
        hess_ref[b] = lax.dot_general(
            jnp.concatenate([tan, act], axis=1),
            jnp.concatenate([pre_grad, pre_tan_grad], axis=1),
            (((1,), (1,)), ((), ())),
            preferred_element_type=jnp.float32,
        ).astype(hess_ref.dtype)
        back_ref[b] = (
            jnp.dot(fac, pre_tan_grad, preferred_element_type=jnp.float32)
            + jnp.dot(fac_tan, pre_grad, preferred_element_type=jnp.float32)
        ).astype(back_ref.dtype)


def mixed_stage(act, tan, grad, fac, fac_tan):
    blocks, width, rows = act.shape
    thin = pl.BlockSpec((STEP, width, rows), lambda s: (s, 0, 0))
    wide = pl.BlockSpec((STEP, width, width), lambda s: (s, 0, 0))
    return pl.pallas_call(
        mixed_kernel,
        grid=(blocks // STEP,),
        in_specs=[thin, thin, thin, wide, wide],
        out_specs=[wide, thin],
        out_shape=[
            jax.ShapeDtypeStruct((blocks, width, width), jnp.bfloat16),
            jax.ShapeDtypeStruct((blocks, width, rows), jnp.bfloat16),
        ],
        compiler_params=pltpu.CompilerParams(vmem_limit_bytes=32 * 1024 * 1024),
        cost_estimate=pl.CostEstimate(
            flops=14 * blocks * width * width * rows,
            bytes_accessed=blocks * width * (6 * width + 8 * rows),
            transcendentals=2 * blocks * width * rows,
        ),
    )(act, tan, grad, fac, fac_tan)


def per_device(
    tokens,
    targets,
    first_blocks,
    second_factor_blocks,
    down_blocks,
    first_tangent,
    second_factor_tangent,
    doc_lengths,
    doc_owners,
    pack_offsets,
):
    loaders = lax.axis_size("dp")
    features = lax.axis_size("feat")
    device = lax.axis_index("dp")
    tok_count, feature_cols = tokens.shape
    pack_rows = targets.shape[0]
    slot_rows = 2 * tok_count // loaders
    local_blocks, block_in, block_out = first_blocks.shape
    all_blocks = local_blocks * features
    local_out = block_out // features
    pair = local_out // local_blocks

    position = jnp.arange(slot_rows, dtype=jnp.int32)
    mine = (doc_owners == device).astype(jnp.int32)
    slot_start = jnp.sum(mine * pack_offsets, axis=1)
    pack_source = jnp.minimum(slot_start[:, None] + position[None, :], pack_rows - 1)
    outgoing = jnp.take(targets, pack_source.reshape(-1), axis=0).reshape(
        loaders, slot_rows, feature_cols
    )
    arrived = lax.all_to_all(outgoing, "dp", split_axis=0, concat_axis=0, tiled=True)
    my_lengths = lax.dynamic_index_in_dim(doc_lengths, device, 0, keepdims=False)
    my_owners = lax.dynamic_index_in_dim(doc_owners, device, 0, keepdims=False)
    my_starts = jnp.cumsum(my_lengths) - my_lengths
    row = jnp.arange(tok_count, dtype=jnp.int32)
    inside = (row[:, None] >= my_starts[None, :]) & (
        row[:, None] < (my_starts + my_lengths)[None, :]
    )
    inside_int = inside.astype(jnp.int32)
    source = jnp.sum(inside_int * (my_owners * slot_rows - my_starts)[None, :], axis=1) + row
    weight = jnp.sum(inside.astype(jnp.float32) / my_lengths.astype(jnp.float32)[None, :], axis=1)
    goal = jnp.take(arrived.reshape(loaders * slot_rows, feature_cols), source, axis=0)

    rows = local_blocks * block_in
    share = rows // loaders
    factors = jnp.stack(
        [
            lax.dynamic_slice_in_dim(w.reshape(rows, block_out), device * share, share, 0)
            for w in (first_blocks, first_tangent, jnp.swapaxes(down_blocks, 1, 2))
        ]
    )
    factors = factors.reshape(3, share, features, local_out).transpose(2, 0, 3, 1)
    factors = lax.all_to_all(factors, "feat", split_axis=0, concat_axis=0, tiled=True)
    factors = lax.all_gather(factors, "dp", axis=0, tiled=False)
    factors = factors.transpose(2, 3, 1, 0, 4).reshape(3, local_out, all_blocks, block_in)

    tok_all = lax.all_gather(tokens, "feat", axis=0, tiled=False)
    tok_all = tok_all.transpose(0, 2, 1).reshape(all_blocks, block_in, tok_count)
    goal_all = lax.all_gather(goal, "feat", axis=0, tiled=False)
    goal_all = goal_all.transpose(0, 2, 1).reshape(all_blocks, block_in, tok_count)

    def mix(values):
        return (
            values.astype(jnp.bfloat16)
            .reshape(all_blocks, local_blocks, pair, tok_count)
            .transpose(1, 0, 2, 3)
            .reshape(local_blocks, block_out, tok_count)
        )

    def first(weights, rows_of):
        return jnp.einsum("jki,kir->kjr", weights, rows_of, preferred_element_type=jnp.float32)

    act = mix(first(factors[0], tok_all))
    tan = mix(first(factors[1], tok_all))
    grad = mix(first(factors[2], goal_all) * weight)
    hess_mixed, back = mixed_stage(act, tan, grad, second_factor_blocks, second_factor_tangent)
    hess_mixed = lax.psum_scatter(hess_mixed, "dp", scatter_dimension=1, tiled=True)

    back = (
        back.reshape(local_blocks, all_blocks, pair, tok_count)
        .transpose(1, 0, 2, 3)
        .reshape(all_blocks, local_out, tok_count)
    )
    hess_first = jnp.einsum("kjr,kir->kij", back, tok_all, preferred_element_type=jnp.float32)
    in_share = block_in // loaders
    hess_first = hess_first.astype(jnp.bfloat16).reshape(
        all_blocks, loaders, in_share * local_out
    )
    hess_first = lax.psum_scatter(
        hess_first.transpose(1, 0, 2), "dp", scatter_dimension=0, tiled=True
    )
    hess_first = hess_first.reshape(features, local_blocks, in_share * local_out)
    hess_first = lax.all_to_all(hess_first, "feat", split_axis=0, concat_axis=0, tiled=True)
    hess_first = (
        hess_first.reshape(features, local_blocks, in_share, local_out)
        .transpose(1, 2, 0, 3)
        .reshape(local_blocks, in_share, block_out)
    )
    return hess_first.astype(jnp.float32), hess_mixed.astype(jnp.float32)


def solution(mesh):
    in_specs = (
        P("dp", "feat"),
        P("dp", "feat"),
        P("feat", None, None),
        P("feat", None, None),
        P("feat", None, None),
        P("feat", None, None),
        P("feat", None, None),
        P(),
        P(),
        P(),
    )
    out_specs = (P("feat", "dp", None), P("feat", "dp", None))
    return jax.shard_map(
        per_device, mesh=mesh, in_specs=in_specs, out_specs=out_specs, check_vma=False
    )
```

time: 628 us -> 303 us (0.48); the launches traced: 620 us -> 303 us
  waiting for transfers between devices: 330 us -> 167 us
  matrix products: 85.8 us -> 12.7 us
  blocking collectives: 95.4 us -> 36.9 us
  local copies, waits for them, and re-layouts: 64.2 us -> 46 us
  starting transfers between devices: 20.8 us -> 5.55 us
  Pallas kernels: 0 us -> 14.4 us
    all_to_all x3 -> x0, waiting for transfers between devices: 226 us -> none  [the longest x1 83.2 us: curvature(): lax.all_to_all(tangents, 'feat', split_axis=0, concat_axis=2, tiled=True)]
    all_gather x0 -> x3, waiting for transfers between devices: none -> 75 us  [the longest x1 43.1 us: per_device(): goal_all = lax.all_gather(goal, 'feat', axis=0, tiled=False)]
    dot_general x11 -> x4, matrix products: 85.8 us -> 12.7 us  [the longest x3 11.4 us: first(): jnp.einsum('jki,kir->kjr', weights, rows_of, preferred_element_type=jnp.f...]
    all_to_all x1 -> x2, blocking collectives: 95.4 us -> 36.9 us  [the longest x1 26.3 us: per_device(): lax.all_to_all(factors, 'feat', split_axis=0, concat_axis=0, tiled=True)]
    reduce_scatter x2, waiting for transfers between devices: 99.8 us -> 77 us  [the longest x1 41.4 us: per_device(): lax.psum_scatter(hess_mixed, 'dp', scatter_dimension=1, tiled=True)]
    all_to_all x3 -> x0, starting transfers between devices: 15.2 us -> none  [the longest x1 5.39 us: curvature(): lax.all_to_all(tangents, 'feat', split_axis=0, concat_axis=2, tiled=True)]
    unnamed x29 -> x14, local copies, waits for them, and re-layouts: 15.7 us -> 0.76 us
    pallas_call x0 -> x1, Pallas kernels: none -> 14.4 us  [mixed_stage(): pl.pallas_call(mixed_kernel, grid=(blocks // STEP,), in_specs=[thin, thin...]
  transfers between devices with their start and end apart: 6 -> 6, of which waited for: 6 -> 6; matrix products, arithmetic and copies ran while one was open for 13% -> 7% of each run, Pallas kernels for 0% -> 0%
where the time goes in v1:
time: 303 us
  waiting for transfers between devices  167 us (55%)
  local copies, waits for them, and re-layouts  46 us (15%)
  blocking collectives  36.9 us (12%)
  Pallas kernels  14.4 us (5%)
  between operations  14 us (5%)
  matrix products  12.7 us (4%)
  other arithmetic  6.3 us (2%)
  starting transfers between devices  5.55 us (2%)
    all_gather x1, waiting for transfers between devices, per_device(): goal_all = lax.all_gather(goal, 'feat', axis=0, tiled=False)  43.1 us
    reduce_scatter x1, waiting for transfers between devices, per_device(): lax.psum_scatter(hess_mixed, 'dp', scatter_dimension=1, tiled=True)  41.4 us
    reduce_scatter x1, waiting for transfers between devices, per_device(): lax.psum_scatter(hess_first.transpose(1, 0, 2), 'dp', scatter_dimension=0...  35.6 us
    all_gather x1, waiting for transfers between devices, per_device(): factors = lax.all_gather(factors, 'dp', axis=0, tiled=False)  29.9 us
    all_to_all x1, blocking collectives, per_device(): lax.all_to_all(factors, 'feat', split_axis=0, concat_axis=0, tiled=True)  26.3 us
    pallas_call x1, Pallas kernels, mixed_stage(): pl.pallas_call(mixed_kernel, grid=(blocks // STEP,), in_specs=[thin, thin...  14.4 us
    all_to_all x1, waiting for transfers between devices, per_device(): lax.all_to_all(outgoing, 'dp', split_axis=0, concat_axis=0, tiled=True)  13.7 us
    dot_general x3, matrix products, first(): jnp.einsum('jki,kir->kjr', weights, rows_of, preferred_element_type=jnp.f...  11.4 us
  transfers between devices with their start and end apart: 6, of which 6 were waited for; matrix products, arithmetic and copies ran while one was open for 7% of the time, Pallas kernels for 0%

profile of v1, /device:TPU:0, one launch (start us, length us, event | category | flops | bytes accessed | tf_op | source)
XLA Modules:
  0.0 302.7 jit_solution(5684447445879862988)
XLA Ops:
  8.9 3.7 %gather_fusion = bf16[256,2048]{1,0:T(8,128)(2,1)S(1)} fusion(bf16[256,2048]{1,0:T(8,128)(2,1)} %param.11, s32[1024]{0:T(1024)S(1)} %pad_clamp_fusion.1), kind=kCustom, calls=%fused_computation | custom fusion | bytes 2098176 | tf_op jit(solution)/shard_map/jit(_take)/gather | solution.py:99
  12.7 1.1 broadcast_select_fusion
  13.9 5.2 %all-to-all-start.1 = ((bf16[8,32,2048]{2,1,0:T(8,128)(2,1)}), bf16[8,32,2048]{2,1,0:T(8,128)(2,1)S(1)}, u32[]{:S(2)}, u32[]{:S(2)}) async-start(bf16[8,32,2048]{2,1,0:T(8,128)(2,1)} %broadcast_select_fusion), calls=%async_computation.1 | async-start | bytes 2097152 | tf_op jit(solution)/shard_map/all_to_all | solution.py:102
  20.8 13.7 %all-to-all-done.1 = bf16[8,32,2048]{2,1,0:T(8,128)(2,1)S(1)} async-done(((bf16[8,32,2048]{2,1,0:T(8,128)(2,1)}), bf16[8,32,2048]{2,1,0:T(8,128)(2,1)S(1)}, u32[]{:S(2)}, u32[]{:S(2)}) %all-to-all-start.1) | async-done | bytes 1048608 | tf_op jit(solution)/shard_map/all_to_all | solution.py:102
  36.5 1.0 constant_dynamic-slice_fusion.2
  37.8 26.3 %all_to_all.15 = bf16[4,3,64,256]{3,2,1,0:T(8,128)(2,1)} all-to-all(bf16[4,3,64,256]{3,2,1,0:T(8,128)(2,1)S(1)} %copy.86), channel_id=1, replica_groups=mesh['dp'=8,'feat'=4] {'feat'}, dimensions={0} | all-to-all | bytes 786432 | tf_op jit(solution)/shard_map/all_to_all | solution.py:124
  64.4 2.0 all-gather.10.cloned.1.call-done
  66.4 3.9 %copy.88 = bf16[4,128,2048]{1,2,0:T(8,128)(2,1)} copy(bf16[4,128,2048]{2,1,0:T(8,128)(2,1)} %bitcast.99) | data formatting | bytes 4194304 | tf_op jit(solution)/shard_map/all_gather | solution.py:128
  70.4 43.1 %all-gather.6.cloned.1.call-done = bf16[4,128,2048]{2,1,0:T(8,128)(2,1)} async-done(((bf16[1,128,2048]{2,1,0:T(8,128)(2,1)}), bf16[4,128,2048]{2,1,0:T(8,128)(2,1)}) %all-gather.6.cloned.1.call-update) | async-done | bytes 2097168 | tf_op jit(solution)/shard_map/all_gather | solution.py:130
  113.4 3.0 %copy.93 = bf16[4,2048,128]{2,1,0:T(8,128)(2,1)S(1)} copy(bf16[4,2048,128]{1,2,0:T(8,128)(2,1)} %bitcast.100) | data formatting | bytes 4194304 | tf_op jit(solution)/shard_map/transpose | solution.py:131
  116.5 29.9 %all-gather.8.cloned.1.call-done = bf16[32,3,64,256]{3,2,1,0:T(8,128)(2,1)} async-done(((bf16[4,3,64,256]{3,2,1,0:T(8,128)(2,1)}), bf16[32,3,64,256]{3,2,1,0:T(8,128)(2,1)}) %all-gather.8.cloned.1.call-update) | async-done | bytes 3145744 | tf_op jit(solution)/shard_map/all_gather | solution.py:125
  146.4 3.7 %copy.111 = bf16[8,4,3,64,256]{4,0,1,3,2:T(8,128)(2,1)S(1)} copy(bf16[8,4,3,64,256]{4,3,2,1,0:T(8,128)(2,1)} %bitcast.97) | data formatting | bytes 6291456 | tf_op jit(solution)/shard_map/all_gather | solution.py:125
  150.1 1.6 fusion.18
  151.7 3.8 %squeeze.14 = bf16[64,128,64]{2,1,0:T(8,128)(2,1)} reshape(bf16[1,64,4,8,256]{4,3,2,1,0:T(8,128)(2,1)} %get-tuple-element.6) | data formatting | bytes 2097152 | tf_op jit(solution)/shard_map/squeeze | solution.py:146
  155.5 3.3 %multiply_convert_fusion = bf16[128,64,128]{2,1,0:T(8,128)(2,1)S(1)} fusion(bf16[128,64,128]{2,1,0:T(8,128)(2,1)S(1)} %bitcast.90, bf16[64,128,64]{2,1,0:T(8,128)(2,1)} %squeeze.14, f32[128]{0:T(128)S(1)} %divide_reduce_fusion), kind=kOutput, calls=%fused_computation.2 | convolution fusion | flops 136314880 | bytes 5243392 | tf_op jit(solution)/shard_map/jki,kir->kjr/dot_general | solution.py:142
  158.9 2.2 copy.95
  161.1 3.8 %squeeze.13 = bf16[64,128,64]{2,1,0:T(8,128)(2,1)} reshape(bf16[1,64,4,8,256]{4,3,2,1,0:T(8,128)(2,1)} %get-tuple-element.7) | data formatting | bytes 2097152 | tf_op jit(solution)/shard_map/squeeze | solution.py:145
  164.9 4.0 %fusion.8 = bf16[128,64,128]{2,1,0:T(8,128)(2,1)S(1)} fusion(bf16[128,64,128]{2,1,0:T(8,128)(2,1)} %bitcast.85, bf16[64,128,64]{2,1,0:T(8,128)(2,1)} %squeeze.13), kind=kOutput, calls=%fused_computation.11 | convolution fusion | flops 135266304 | bytes 5242880 | tf_op jit(solution)/shard_map/jki,kir->kjr/dot_general | solution.py:142
  168.9 3.6 %copy.92 = bf16[128,32,2,128]{3,2,0,1:T(2,128)(2,1)} copy(bf16[128,32,2,128]{3,2,1,0:T(2,128)(2,1)S(1)} %bitcast.93) | data formatting | bytes 4194304 | tf_op jit(solution)/shard_map/reshape | solution.py:136
  172.4 1.8 squeeze.12
  174.3 4.1 %fusion.5 = bf16[128,64,128]{2,1,0:T(8,128)(2,1)S(1)} fusion(bf16[128,64,128]{2,1,0:T(8,128)(2,1)} %bitcast.86, bf16[64,128,64]{2,1,0:T(8,128)(2,1)} %squeeze.12), kind=kOutput, calls=%fused_computation.10 | convolution fusion | flops 135266304 | bytes 5242880 | tf_op jit(solution)/shard_map/jki,kir->kjr/dot_general | solution.py:142
  178.4 2.2 copy.90
  180.6 14.4 %shard_map.113 = (bf16[32,256,256]{2,1,0:T(8,128)(2,1)S(1)}, bf16[32,256,128]{2,1,0:T(8,128)(2,1)S(1)}) custom-call(bf16[32,256,128]{2,1,0:T(8,128)(2,1)S(1)} %bitcast.83, bf16[32,256,128]{2,1,0:T(8,128)(2,1)S(1)} %bitcast.82, bf16[32,256,128]{2,1,0:T(8,128)(2,1)S(1)} %bitcast.81, bf16[32,256,256]{2,1,0:T(8,128)(2,1)S(1)} %copy-done.3, ...), custom_call_target="tpu_custom_call" | custom-call | flops 3758096384 | bytes 20971520 | tf_op jit(solution)/shard_map/pallas_call | solution.py:54
  195.0 2.4 copy.96
  198.1 1.2 convert_bitcast_fusion
  199.3 3.9 %copy.97 = bf16[128,64,64]{0,2,1:T(8,128)(2,1)} copy(bf16[128,64,64]{1,2,0:T(8,128)(2,1)S(1)} %convert_bitcast_fusion) | data formatting | bytes 2097152 | tf_op jit(solution)/shard_map/convert_element_type | solution.py:157
  203.9 35.6 %reduce-scatter.3.cloned.1.call-done = bf16[1,128,512]{1,2,0:T(8,128)(2,1)} async-done(((bf16[8,128,512]{1,2,0:T(8,128)(2,1)}), bf16[1,128,512]{1,2,0:T(8,128)(2,1)}) %reduce-scatter.3.cloned.1.call-update) | async-done | bytes 131088 | tf_op jit(solution)/shard_map/reduce_scatter | solution.py:160
  239.5 1.0 copy.98
  240.5 10.6 %all_to_all.16 = bf16[4,32,512]{2,1,0:T(8,128)(2,1)S(1)} all-to-all(bf16[4,32,512]{2,1,0:T(8,128)(2,1)S(1)} %bitcast.101), channel_id=1, replica_groups=mesh['dp'=8,'feat'=4] {'feat'}, dimensions={0} | all-to-all | bytes 262144 | tf_op jit(solution)/shard_map/all_to_all | solution.py:164
  251.6 1.0 reshape.198
  252.6 41.4 %reduce-scatter.5.cloned.1.call-done = bf16[32,32,256]{2,1,0:T(8,128)(2,1)} async-done(((bf16[32,256,256]{2,1,0:T(8,128)(2,1)}), bf16[32,32,256]{2,1,0:T(8,128)(2,1)}) %reduce-scatter.5.cloned.1.call-update) | async-done | bytes 524304 | tf_op jit(solution)/shard_map/reduce_scatter | solution.py:148
  294.0 2.1 convert_element_type.50
  (48 shorter events, 8.0 us)
Async XLA Ops:
  7.2 29.2 %copy-start = (bf16[32,64,256]{2,1,0:T(8,128)(2,1)S(1)}, bf16[32,64,256]{2,1,0:T(8,128)(2,1)}, u32[]{:S(2)}) copy-start(bf16[32,64,256]{2,1,0:T(8,128)(2,1)} %param.12) | copy-start | bytes 3145732
  7.2 59.2 %all-gather.10.cloned.1.call-start = ((), (), s32[]{:S(2)}) async-start(), calls=%async_computation.9 | async-start | bytes 2621440 | tf_op jit(solution)/shard_map/all_gather | solution.py:128
  13.9 20.6 %all-to-all-start.1 = ((bf16[8,32,2048]{2,1,0:T(8,128)(2,1)}), bf16[8,32,2048]{2,1,0:T(8,128)(2,1)S(1)}, u32[]{:S(2)}, u32[]{:S(2)}) async-start(bf16[8,32,2048]{2,1,0:T(8,128)(2,1)} %broadcast_select_fusion), calls=%async_computation.1 | async-start | bytes 2097152 | tf_op jit(solution)/shard_map/all_to_all | solution.py:102
  19.0 94.4 %all-gather.6.cloned.1.call-start = ((), (), s32[]{:S(2)}) async-start(), calls=%async_computation.5 | async-start | bytes 2621440 | tf_op jit(solution)/shard_map/all_gather | solution.py:130
  36.3 110.1 %all-gather.8.cloned.1.call-start = ((), (), s32[]{:S(2)}) async-start(), calls=%async_computation.8 | async-start | bytes 3538944 | tf_op jit(solution)/shard_map/all_gather | solution.py:125
  64.1 175.4 %reduce-scatter.3.cloned.1.call-start = ((), (), s32[]{:S(2)}) async-start(), calls=%async_computation.6 | async-start | bytes 1179648 | tf_op jit(solution)/shard_map/reduce_scatter | solution.py:160
  174.3 6.3 %copy-start.3 = (bf16[32,256,256]{2,1,0:T(8,128)(2,1)S(1)}, bf16[32,256,256]{2,1,0:T(8,128)(2,1)}, u32[]{:S(2)}) copy-start(bf16[32,256,256]{2,1,0:T(8,128)(2,1)} %fac_ref.1) | copy-start | bytes 12582916
  174.3 6.3 %copy-start.4 = (bf16[32,256,256]{2,1,0:T(8,128)(2,1)S(1)}, bf16[32,256,256]{2,1,0:T(8,128)(2,1)}, u32[]{:S(2)}) copy-start(bf16[32,256,256]{2,1,0:T(8,128)(2,1)} %fac_tan_ref.1) | copy-start | bytes 12582916
  178.4 2.2 copy-start.2
  195.0 2.4 copy-start.5
  195.0 3.1 %copy-start.6 = (bf16[4,128,2048]{1,2,0:T(8,128)(2,1)S(1)}, bf16[4,128,2048]{1,2,0:T(8,128)(2,1)}, u32[]{:S(2)}) copy-start(bf16[4,128,2048]{1,2,0:T(8,128)(2,1)} %copy.88) | copy-start | bytes 6291460
  203.3 90.7 %reduce-scatter.5.cloned.1.call-start = ((), (), s32[]{:S(2)}) async-start(), calls=%async_computation.7 | async-start | bytes 4718592 | tf_op jit(solution)/shard_map/reduce_scatter | solution.py:148
  240.5 55.7 %copy-start.1 = (bf16[32,64,256]{2,1,0:T(8,128)(2,1)S(1)}, bf16[32,64,256]{2,1,0:T(8,128)(2,1)}, u32[]{:S(2)}) copy-start(bf16[32,64,256]{2,1,0:T(8,128)(2,1)} %param.12) | copy-start | bytes 3145732
Sparse Core Ops, SparseCore 0:
  9.6 56.7 all-gather.9
  68.6 44.8 all-gather.5
  115.3 31.0 all-gather.7
  203.4 36.0 reduce-scatter.2
  242.7 51.2 reduce-scatter.4

commit v2 on v1

--- a/solution.py
+++ b/solution.py
@@ -1,3 +1,5 @@
+import functools
+
 import jax
 import jax.numpy as jnp
 from jax import lax
@@ -8,6 +10,252 @@
 inv_root_two = 0.7071067811865476
 inv_root_two_pi = 0.3989422804014327
 STEP = 2
+MESH = pl.DeviceIdType.MESH
+
+
+def column_loop(columns, body):
+    tile = min(columns, 256)
+
+    @pl.loop(0, columns // tile)
+    def _(step):
+        body(pl.ds(pl.multiple_of(step * tile, tile), tile))
+
+
+def gather_kernel(
+    loaders,
+    features,
+    tok_ref,
+    target_ref,
+    send_sel_ref,
+    take_sel_ref,
+    fac_ref,
+    tok_all,
+    goal_all,
+    fac_all,
+    outgoing,
+    arrived,
+    slot_send,
+    slot_recv,
+    fac_send,
+    fac_recv,
+    chip_send,
+    chip_recv,
+    pair_send,
+    pair_recv,
+    line_send,
+    line_recv,
+):
+    dev = lax.axis_index("dp")
+    me = lax.axis_index("feat")
+    columns = tok_ref.shape[1]
+    slot = outgoing.shape[0] // loaders
+
+    def to_dp(peer):
+        return {"dp": peer}
+
+    def to_feat(peer):
+        return {"feat": peer}
+
+    barrier = pltpu.get_barrier_semaphore()
+    for off in range(1, loaders):
+        pl.semaphore_signal(
+            barrier, inc=1, device_id=to_dp(lax.rem(dev + off, loaders)), device_id_type=MESH
+        )
+    for off in range(1, features):
+        pl.semaphore_signal(
+            barrier, inc=1, device_id=to_feat(lax.rem(me + off, features)), device_id_type=MESH
+        )
+    pl.semaphore_wait(barrier, loaders + features - 2)
+
+    def remote(src, dst, send, recv, target):
+        return pltpu.make_async_remote_copy(
+            src_ref=src,
+            dst_ref=dst,
+            send_sem=send,
+            recv_sem=recv,
+            device_id=target,
+            device_id_type=MESH,
+        )
+
+    fac_copies = []
+    for off in range(1, features):
+        peer = lax.rem(me + off, features)
+        fac_copies.append(
+            remote(
+                fac_ref.at[peer],
+                fac_all.at[dev, me],
+                fac_send.at[off - 1],
+                fac_recv.at[off - 1],
+                to_feat(peer),
+            )
+        )
+        fac_copies[-1].start()
+    fac_all[dev, me] = fac_ref[me]
+
+    def hop(ref, which, step, right):
+        shard = jnp.maximum(me - step, 0) if right else jnp.minimum(me + step, features - 1)
+        peer = jnp.minimum(me + 1, features - 1) if right else jnp.maximum(me - 1, 0)
+        side = 0 if right else 1
+        return remote(
+            ref.at[shard],
+            ref.at[shard],
+            line_send.at[which, side, step],
+            line_recv.at[which, side, step],
+            to_feat(peer),
+        )
+
+    def has(step, right):
+        return (me >= step) if right else (me + step <= features - 1)
+
+    def sends(step, right):
+        return has(step, right) & ((me < features - 1) if right else (me > 0))
+
+    def line_step(ref, which, step):
+        for right in (True, False):
+            if step > 0:
+
+                @pl.when(has(step, right))
+                def _():
+                    hop(ref, which, step - 1, right).wait_recv()
+
+            if step < features - 1:
+
+                @pl.when(sends(step, right))
+                def _():
+                    hop(ref, which, step, right).start()
+
+    def line_end(ref, which):
+        for step in range(features - 1):
+            for right in (True, False):
+
+                @pl.when(sends(step, right))
+                def _():
+                    hop(ref, which, step, right).wait_send()
+
+    def turn_tokens(cols):
+        tok_all[me, cols, :] = tok_ref[:, cols].T
+
+    column_loop(columns, turn_tokens)
+    line_step(tok_all, 0, 0)
+
+    def pick(cols):
+        outgoing[:, cols] = jnp.dot(
+            send_sel_ref[...], target_ref[:, cols], preferred_element_type=jnp.float32
+        ).astype(jnp.bfloat16)
+
+    column_loop(columns, pick)
+    slot_copies = []
+    for off in range(1, loaders):
+        peer = lax.rem(dev + off, loaders)
+        slot_copies.append(
+            remote(
+                outgoing.at[pl.ds(pl.multiple_of(peer * slot, slot), slot)],
+                arrived.at[pl.ds(pl.multiple_of(dev * slot, slot), slot)],
+                slot_send.at[off - 1],
+                slot_recv.at[off - 1],
+                to_dp(peer),
+            )
+        )
+        slot_copies[-1].start()
+    own = pl.ds(pl.multiple_of(dev * slot, slot), slot)
+    arrived[own] = outgoing[own]
+
+    for copy in fac_copies:
+        copy.wait_recv()
+    chips = loaders // 2
+    chip = dev // 2
+    core = lax.rem(dev, 2)
+    sibling = dev + 1 - 2 * core
+
+    def to_pair(index, piece):
+        return remote(
+            fac_all.at[piece],
+            fac_all.at[piece],
+            pair_send.at[index],
+            pair_recv.at[index],
+            to_dp(sibling),
+        )
+
+    pair_copies = [to_pair(0, dev)]
+    pair_copies[0].start()
+    chip_copies = []
+    for off in range(1, chips):
+        peer = lax.rem(chip + off, chips) * 2 + core
+        chip_copies.append(
+            remote(
+                fac_all.at[dev],
+                fac_all.at[dev],
+                chip_send.at[off - 1],
+                chip_recv.at[off - 1],
+                to_dp(peer),
+            )
+        )
+        chip_copies[-1].start()
+
+    if features > 2:
+        line_step(tok_all, 0, 1)
+    for copy in slot_copies:
+        copy.wait_recv()
+
+    def take(cols):
+        goal_all[me, cols, :] = lax.dot_general(
+            arrived[:, cols],
+            take_sel_ref[...],
+            (((0,), (0,)), ((), ())),
+            preferred_element_type=jnp.float32,
+        ).astype(jnp.bfloat16)
+
+    column_loop(columns, take)
+    line_step(goal_all, 1, 0)
+    for step in range(2, features):
+        line_step(tok_all, 0, step)
+    for off in range(1, chips):
+        chip_copies[off - 1].wait_recv()
+        piece = lax.rem(chip + chips - off, chips) * 2 + core
+        pair_copies.append(to_pair(off, piece))
+        pair_copies[-1].start()
+    for step in range(1, features):
+        line_step(goal_all, 1, step)
+    for copy in pair_copies:
+        copy.wait()
+    for copy in slot_copies + fac_copies + chip_copies:
+        copy.wait_send()
+    line_end(tok_all, 0)
+    line_end(goal_all, 1)
+
+
+def gather_stage(loaders, features, tokens, targets, send_sel, take_sel, factors):
+    rows, columns = tokens.shape
+    slots = send_sel.shape[0]
+    dma = pltpu.SemaphoreType.DMA
+    vmem = pl.BlockSpec(memory_space=pltpu.VMEM)
+    return pl.pallas_call(
+        functools.partial(gather_kernel, loaders, features),
+        in_specs=[vmem] * 5,
+        out_specs=[vmem] * 3,
+        out_shape=[
+            jax.ShapeDtypeStruct((features, columns, rows), jnp.bfloat16),
+            jax.ShapeDtypeStruct((features, columns, rows), jnp.bfloat16),
+            jax.ShapeDtypeStruct((loaders,) + factors.shape, jnp.bfloat16),
+        ],
+        scratch_shapes=[
+            pltpu.VMEM((slots, columns), jnp.bfloat16),
+            pltpu.VMEM((slots, columns), jnp.bfloat16),
+            dma((loaders - 1,)),
+            dma((loaders - 1,)),
+            dma((features - 1,)),
+            dma((features - 1,)),
+            dma((loaders // 2 - 1,)),
+            dma((loaders // 2 - 1,)),
+            dma((loaders // 2,)),
+            dma((loaders // 2,)),
+            dma((2, 2, features - 1)),
+            dma((2, 2, features - 1)),
+        ],
+        compiler_params=pltpu.CompilerParams(
+            collective_id=0, has_side_effects=True, vmem_limit_bytes=48 * 1024 * 1024
+        ),
+    )(tokens, targets, send_sel, take_sel, factors)
 
 
 def mixed_kernel(act_ref, tan_ref, grad_ref, fac_ref, fac_tan_ref, hess_ref, back_ref):
@@ -86,7 +334,7 @@
     device = lax.axis_index("dp")
     tok_count, feature_cols = tokens.shape
     pack_rows = targets.shape[0]
-    slot_rows = 2 * tok_count // loaders
+    slot_rows = -(-2 * tok_count // (16 * loaders)) * 16
     local_blocks, block_in, block_out = first_blocks.shape
     all_blocks = local_blocks * features
     local_out = block_out // features
@@ -95,11 +343,10 @@
     position = jnp.arange(slot_rows, dtype=jnp.int32)
     mine = (doc_owners == device).astype(jnp.int32)
     slot_start = jnp.sum(mine * pack_offsets, axis=1)
-    pack_source = jnp.minimum(slot_start[:, None] + position[None, :], pack_rows - 1)
-    outgoing = jnp.take(targets, pack_source.reshape(-1), axis=0).reshape(
-        loaders, slot_rows, feature_cols
-    )
-    arrived = lax.all_to_all(outgoing, "dp", split_axis=0, concat_axis=0, tiled=True)
+    pack_source = (slot_start[:, None] + position[None, :]).reshape(-1)
+    send_sel = (
+        pack_source[:, None] == jnp.arange(pack_rows, dtype=jnp.int32)[None, :]
+    ).astype(jnp.bfloat16)
     my_lengths = lax.dynamic_index_in_dim(doc_lengths, device, 0, keepdims=False)
     my_owners = lax.dynamic_index_in_dim(doc_owners, device, 0, keepdims=False)
     my_starts = jnp.cumsum(my_lengths) - my_lengths
@@ -110,7 +357,9 @@
     inside_int = inside.astype(jnp.int32)
     source = jnp.sum(inside_int * (my_owners * slot_rows - my_starts)[None, :], axis=1) + row
     weight = jnp.sum(inside.astype(jnp.float32) / my_lengths.astype(jnp.float32)[None, :], axis=1)
-    goal = jnp.take(arrived.reshape(loaders * slot_rows, feature_cols), source, axis=0)
+    take_sel = (
+        jnp.arange(loaders * slot_rows, dtype=jnp.int32)[:, None] == source[None, :]
+    ).astype(jnp.bfloat16)
 
     rows = local_blocks * block_in
     share = rows // loaders
@@ -121,14 +370,14 @@
         ]
     )
     factors = factors.reshape(3, share, features, local_out).transpose(2, 0, 3, 1)
-    factors = lax.all_to_all(factors, "feat", split_axis=0, concat_axis=0, tiled=True)
-    factors = lax.all_gather(factors, "dp", axis=0, tiled=False)
+    factors = factors.reshape(features, 3 * local_out, share)
+    tok_all, goal_all, factors = gather_stage(
+        loaders, features, tokens, targets, send_sel, take_sel, factors
+    )
+    factors = factors.reshape(loaders, features, 3, local_out, share)
     factors = factors.transpose(2, 3, 1, 0, 4).reshape(3, local_out, all_blocks, block_in)
-
-    tok_all = lax.all_gather(tokens, "feat", axis=0, tiled=False)
-    tok_all = tok_all.transpose(0, 2, 1).reshape(all_blocks, block_in, tok_count)
-    goal_all = lax.all_gather(goal, "feat", axis=0, tiled=False)
-    goal_all = goal_all.transpose(0, 2, 1).reshape(all_blocks, block_in, tok_count)
+    tok_all = tok_all.reshape(all_blocks, block_in, tok_count)
+    goal_all = goal_all.reshape(all_blocks, block_in, tok_count)
 
     def mix(values):
         return (

time: 303 us -> 262 us (0.86)
  waiting for transfers between devices: 167 us -> 75.6 us
  Pallas kernels: 14.4 us -> 102 us
  blocking collectives: 36.9 us -> 10.5 us
  starting transfers between devices: 5.55 us -> 0.08 us
  local copies, waits for them, and re-layouts: 46 us -> 41.8 us
    pallas_call x0 -> x1, Pallas kernels: none -> 87.3 us  [gather_stage(): pl.pallas_call(functools.partial(gather_kernel, loaders, features), in_sp...]
    all_gather x3 -> x0, waiting for transfers between devices: 75 us -> none  [the longest x1 43.1 us: per_device(): goal_all = lax.all_gather(goal, 'feat', axis=0, tiled=False)]
    all_to_all x1 -> x0, blocking collectives: 26.3 us -> none  [per_device(): lax.all_to_all(factors, 'feat', split_axis=0, concat_axis=0, tiled=True)]
    all_to_all x1 -> x0, waiting for transfers between devices: 13.7 us -> none  [per_device(): lax.all_to_all(outgoing, 'dp', split_axis=0, concat_axis=0, tiled=True)]
    all_gather x2 -> x0, local copies, waits for them, and re-layouts: 7.6 us -> none  [the longest x1 3.93 us: per_device(): tok_all = lax.all_gather(tokens, 'feat', axis=0, tiled=False)]
    all_to_all x1 -> x0, starting transfers between devices: 5.17 us -> none  [per_device(): lax.all_to_all(outgoing, 'dp', split_axis=0, concat_axis=0, tiled=True)]
    gather x2 -> x0, local copies, waits for them, and re-layouts: 4.66 us -> none  [the longest x1 3.72 us: per_device(): jnp.take(targets, pack_source.reshape(-1), axis=0)]
    reshape x1 -> x2, local copies, waits for them, and re-layouts: 0.7 us -> 4.45 us  [the longest x1 3.68 us: per_device(): factors = factors.reshape(loaders, features, 3, local_out, share)]
  transfers between devices with their start and end apart: 6 -> 2, of which waited for: 6 -> 2; matrix products, arithmetic and copies ran while one was open for 7% -> 1% of each run, Pallas kernels for 0% -> 0%
where the time goes in v2:
time: 262 us; the launch traced here: 261 us
  Pallas kernels  102 us (39%)
  waiting for transfers between devices  75.6 us (29%)
  local copies, waits for them, and re-layouts  41.8 us (16%)
  between operations  14.2 us (5%)
  matrix products  13.2 us (5%)
  blocking collectives  10.5 us (4%)
  other arithmetic  4.26 us (2%)
    pallas_call x1, Pallas kernels, gather_stage(): pl.pallas_call(functools.partial(gather_kernel, loaders, features), in_sp...  87.3 us
    reduce_scatter x1, waiting for transfers between devices, per_device(): lax.psum_scatter(hess_mixed, 'dp', scatter_dimension=1, tiled=True)  41.7 us
    reduce_scatter x1, waiting for transfers between devices, per_device(): lax.psum_scatter(hess_first.transpose(1, 0, 2), 'dp', scatter_dimension=0...  33.3 us
    pallas_call x1, Pallas kernels, mixed_stage(): pl.pallas_call(mixed_kernel, grid=(blocks // STEP,), in_specs=[thin, thin...  14.4 us
    dot_general x3, matrix products, first(): jnp.einsum('jki,kir->kjr', weights, rows_of, preferred_element_type=jnp.f...  10.7 us
    all_to_all x1, blocking collectives, per_device(): lax.all_to_all(hess_first, 'feat', split_axis=0, concat_axis=0, tiled=True)  10.5 us
    reshape x3, local copies, waits for them, and re-layouts, mix(): return values.astype(jnp.bfloat16).reshape(all_blocks, local_blocks, pair...  9.28 us
  transfers between devices with their start and end apart: 2, of which 2 were waited for; matrix products, arithmetic and copies ran while one was open for 1% of the time, Pallas kernels for 0%

profile of v2, /device:TPU:0, one launch (start us, length us, event | category | flops | bytes accessed | tf_op | source)
XLA Modules:
  0.0 261.3 jit_solution(3770087227187204033)
XLA Ops:
  7.2 0.8 fusion.18
  8.0 0.2 reduce-window.4
  8.2 0.8 select_reduce_fusion.1
  9.0 0.7 fusion.17
  10.3 1.0 constant_dynamic-slice_fusion
  11.6 1.2 copy-done.6
  12.8 1.0 copy-done.7
  13.9 87.3 %shard_map.113 = (bf16[4,2048,128]{2,1,0:T(8,128)(2,1)S(1)}, bf16[4,2048,128]{2,1,0:T(8,128)(2,1)}, bf16[8,4,192,256]{3,2,1,0:T(8,128)(2,1)}) custom-call(bf16[128,2048]{1,0:T(8,128)(2,1)S(1)} %copy-done.7, bf16[256,2048]{1,0:T(8,128)(2,1)S(1)} %copy-done.6, bf16[256,256]{1,0:T(8,128)(2,1)S(1)} %fusion.11.send_sel_ref, ...), custom_call_target="tpu_custom_call" | custom-call | tf_op jit(solution)/shard_map/pallas_call | solution.py:232
  101.1 3.7 %copy.71 = bf16[8,4,3,64,256]{4,0,1,3,2:T(8,128)(2,1)S(1)} copy(bf16[8,4,3,64,256]{4,3,2,1,0:T(8,128)(2,1)} %bitcast.79) | data formatting | bytes 6291456 | tf_op jit(solution)/shard_map/reshape | solution.py:377
  104.8 1.8 fusion.19
  106.6 3.9 %squeeze.14 = bf16[64,128,64]{2,1,0:T(8,128)(2,1)} reshape(bf16[1,64,4,8,256]{4,3,2,1,0:T(8,128)(2,1)} %get-tuple-element.12) | data formatting | bytes 2097152 | tf_op jit(solution)/shard_map/squeeze | solution.py:395
  110.4 4.0 %multiply_convert_fusion = bf16[128,64,128]{2,1,0:T(8,128)(2,1)S(1)} fusion(bf16[128,64,128]{2,1,0:T(8,128)(2,1)} %bitcast.80, bf16[64,128,64]{2,1,0:T(8,128)(2,1)} %squeeze.14, f32[128]{0:T(128)S(1)} %divide_reduce_fusion), kind=kOutput, calls=%fused_computation | convolution fusion | flops 136314880 | bytes 5243392 | tf_op jit(solution)/shard_map/jki,kir->kjr/dot_general | solution.py:391
  114.4 3.6 %copy.55 = bf16[128,32,2,128]{3,2,0,1:T(2,128)(2,1)} copy(bf16[128,32,2,128]{3,2,1,0:T(2,128)(2,1)S(1)} %bitcast.74) | data formatting | bytes 4194304 | tf_op jit(solution)/shard_map/reshape | solution.py:385
  118.0 3.8 %squeeze.13 = bf16[64,128,64]{2,1,0:T(8,128)(2,1)} reshape(bf16[1,64,4,8,256]{4,3,2,1,0:T(8,128)(2,1)} %get-tuple-element.13) | data formatting | bytes 2097152 | tf_op jit(solution)/shard_map/squeeze | solution.py:394
  121.8 3.3 %fusion.8 = bf16[128,64,128]{2,1,0:T(8,128)(2,1)S(1)} fusion(bf16[128,64,128]{2,1,0:T(8,128)(2,1)S(1)} %bitcast.65, bf16[64,128,64]{2,1,0:T(8,128)(2,1)} %squeeze.13), kind=kOutput, calls=%fused_computation.8 | convolution fusion | flops 135266304 | bytes 5242880 | tf_op jit(solution)/shard_map/jki,kir->kjr/dot_general | solution.py:391
  125.1 3.5 %copy.53 = bf16[128,32,2,128]{3,2,0,1:T(2,128)(2,1)} copy(bf16[128,32,2,128]{3,2,1,0:T(2,128)(2,1)S(1)} %bitcast.76) | data formatting | bytes 4194304 | tf_op jit(solution)/shard_map/reshape | solution.py:385
  128.6 3.8 %squeeze.12 = bf16[64,128,64]{2,1,0:T(8,128)(2,1)} reshape(bf16[1,64,4,8,256]{4,3,2,1,0:T(8,128)(2,1)} %get-tuple-element.14) | data formatting | bytes 2097152 | tf_op jit(solution)/shard_map/squeeze | solution.py:393
  132.4 3.4 %fusion.5 = bf16[128,64,128]{2,1,0:T(8,128)(2,1)S(1)} fusion(bf16[128,64,128]{2,1,0:T(8,128)(2,1)S(1)} %bitcast.66, bf16[64,128,64]{2,1,0:T(8,128)(2,1)} %squeeze.12), kind=kOutput, calls=%fused_computation.7 | convolution fusion | flops 135266304 | bytes 5242880 | tf_op jit(solution)/shard_map/jki,kir->kjr/dot_general | solution.py:391
  135.9 2.2 copy.51
  138.1 2.2 copy-done.4
  140.3 14.4 %shard_map.114 = (bf16[32,256,256]{2,1,0:T(8,128)(2,1)S(1)}, bf16[32,256,128]{2,1,0:T(8,128)(2,1)S(1)}) custom-call(bf16[32,256,128]{2,1,0:T(8,128)(2,1)S(1)} %bitcast.70, bf16[32,256,128]{2,1,0:T(8,128)(2,1)S(1)} %bitcast.69, bf16[32,256,128]{2,1,0:T(8,128)(2,1)S(1)} %bitcast.68, bf16[32,256,256]{2,1,0:T(8,128)(2,1)S(1)} %copy-done.3, ...), custom_call_target="tpu_custom_call" | custom-call | flops 3758096384 | bytes 20971520 | tf_op jit(solution)/shard_map/pallas_call | solution.py:302
  154.7 2.4 copy.56
  157.0 2.6 convolution_convert_fusion
  159.6 4.0 %copy.57 = bf16[128,64,64]{0,2,1:T(8,128)(2,1)} copy(bf16[128,64,64]{2,1,0:T(8,128)(2,1)} %convolution_convert_fusion) | data formatting | bytes 2097152 | tf_op jit(solution)/shard_map/convert_element_type | solution.py:406
  163.7 0.7 reduce-scatter.5.cloned.1.call-update
  164.4 33.3 %reduce-scatter.3.cloned.1.call-done = bf16[1,128,512]{1,2,0:T(8,128)(2,1)} async-done(((bf16[8,128,512]{1,2,0:T(8,128)(2,1)}), bf16[1,128,512]{1,2,0:T(8,128)(2,1)}) %reduce-scatter.3.cloned.1.call-update) | async-done | bytes 131088 | tf_op jit(solution)/shard_map/reduce_scatter | solution.py:409
  197.7 1.0 copy.58
  198.7 10.5 %all_to_all.5 = bf16[4,32,512]{2,1,0:T(8,128)(2,1)S(1)} all-to-all(bf16[4,32,512]{2,1,0:T(8,128)(2,1)S(1)} %bitcast.82), channel_id=1, replica_groups=mesh['dp'=8,'feat'=4] {'feat'}, dimensions={0} | all-to-all | bytes 262144 | tf_op jit(solution)/shard_map/all_to_all | solution.py:413
  209.3 0.3 copy.59
  209.6 1.0 reshape.124
  210.7 41.7 %reduce-scatter.5.cloned.1.call-done = bf16[32,32,256]{2,1,0:T(8,128)(2,1)} async-done(((bf16[32,256,256]{2,1,0:T(8,128)(2,1)}), bf16[32,32,256]{2,1,0:T(8,128)(2,1)}) %reduce-scatter.5.cloned.1.call-update) | async-done | bytes 524304 | tf_op jit(solution)/shard_map/reduce_scatter | solution.py:397
  252.3 2.1 convert_element_type.54
  (29 shorter events, 1.1 us)
Async XLA Ops:
  7.2 3.0 %copy-start = (bf16[32,64,256]{2,1,0:T(8,128)(2,1)S(1)}, bf16[32,64,256]{2,1,0:T(8,128)(2,1)}, u32[]{:S(2)}) copy-start(bf16[32,64,256]{2,1,0:T(8,128)(2,1)} %param.15) | copy-start | bytes 3145732
  7.2 190.5 %reduce-scatter.3.cloned.1.call-start = ((), (), s32[]{:S(2)}) async-start(), calls=%async_computation.3 | async-start | bytes 1179648 | tf_op jit(solution)/shard_map/reduce_scatter | solution.py:409
  11.6 1.2 copy-start.6
  12.8 1.0 copy-start.7
  132.4 5.6 %copy-start.3 = (bf16[32,256,256]{2,1,0:T(8,128)(2,1)S(1)}, bf16[32,256,256]{2,1,0:T(8,128)(2,1)}, u32[]{:S(2)}) copy-start(bf16[32,256,256]{2,1,0:T(8,128)(2,1)} %fac_ref.1) | copy-start | bytes 12582916
  135.9 2.2 copy-start.1
  135.9 2.2 copy-start.2
  138.1 2.2 copy-start.4
  154.7 2.4 copy-start.5
  163.6 88.7 %reduce-scatter.5.cloned.1.call-start = ((), (), s32[]{:S(2)}) async-start(), calls=%async_computation.4 | async-start | bytes 4718592 | tf_op jit(solution)/shard_map/reduce_scatter | solution.py:397
Sparse Core Ops, SparseCore 0:
  163.8 33.8 reduce-scatter.2
  201.0 51.2 reduce-scatter.4

commit v3 on v2

--- a/solution.py
+++ b/solution.py
@@ -258,6 +258,173 @@
     )(tokens, targets, send_sel, take_sel, factors)
 
 
+def reduce_kernel(
+    loaders,
+    features,
+    mix_ref,
+    fir_ref,
+    mix_out,
+    fir_out,
+    mix_pair,
+    fir_pair,
+    mix_sum,
+    fir_sum,
+    mix_got,
+    fir_got,
+    fir_total,
+    pair_send,
+    pair_recv,
+    chip_send,
+    chip_recv,
+    feat_send,
+    feat_recv,
+):
+    dev = lax.axis_index("dp")
+    me = lax.axis_index("feat")
+    chips = loaders // 2
+    chip = dev // 2
+    core = lax.rem(dev, 2)
+    sibling = dev + 1 - 2 * core
+
+    def chip_at(off):
+        return lax.rem(chip + off, chips)
+
+    targets = [{"dp": sibling}]
+    targets += [{"dp": chip_at(off) * 2 + core} for off in range(1, chips)]
+    targets += [{"feat": lax.rem(me + off, features)} for off in range(1, features)]
+    barrier = pltpu.get_barrier_semaphore()
+    for target in targets:
+        pl.semaphore_signal(barrier, inc=1, device_id=target, device_id_type=MESH)
+    pl.semaphore_wait(barrier, len(targets))
+
+    def remote(src, dst, send, recv, target):
+        return pltpu.make_async_remote_copy(
+            src_ref=src,
+            dst_ref=dst,
+            send_sem=send,
+            recv_sem=recv,
+            device_id=target,
+            device_id_type=MESH,
+        )
+
+    parts = ((fir_ref, fir_pair, fir_sum, fir_got), (mix_ref, mix_pair, mix_sum, mix_got))
+    order = list(range(1, chips)) + [0]
+    pairs = {}
+    for which, (ref, pair, _, _) in enumerate(parts):
+        for off in order:
+            there = chip_at(off)
+            pairs[which, off] = remote(
+                ref.at[there * 2 + 1 - core],
+                pair.at[there],
+                pair_send.at[which, off],
+                pair_recv.at[which, off],
+                {"dp": sibling},
+            )
+            pairs[which, off].start()
+
+    def each(count, body):
+        @pl.loop(0, count)
+        def _(index):
+            body(index)
+
+    sent = {}
+    for which, (ref, pair, total, got) in enumerate(parts):
+        for off in range(1, chips):
+            there = chip_at(off)
+            pairs[which, off].wait_recv()
+
+            def add(index):
+                total[there, index] = (
+                    ref[there * 2 + core, index].astype(jnp.float32)
+                    + pair[there, index].astype(jnp.float32)
+                ).astype(jnp.bfloat16)
+
+            each(ref.shape[1], add)
+            sent[which, off] = remote(
+                total.at[there],
+                got.at[off - 1],
+                chip_send.at[which, off - 1],
+                chip_recv.at[which, off - 1],
+                {"dp": there * 2 + core},
+            )
+            sent[which, off].start()
+
+    def finish(which, store):
+        ref, pair, _, got = parts[which]
+        pairs[which, 0].wait_recv()
+        for off in range(1, chips):
+            sent[which, off].wait_recv()
+
+        def add(index):
+            value = ref[dev, index].astype(jnp.float32) + pair[chip, index].astype(jnp.float32)
+            for off in range(1, chips):
+                value = value + got[off - 1, index].astype(jnp.float32)
+            store(index, value)
+
+        each(ref.shape[1], add)
+
+    def store_first(index, value):
+        fir_total[index] = value.astype(jnp.bfloat16)
+
+    def store_mixed(index, value):
+        mix_out[index] = value
+
+    finish(0, store_first)
+    last = []
+    for off in range(1, features):
+        peer = lax.rem(me + off, features)
+        last.append(
+            remote(
+                fir_total.at[peer],
+                fir_out.at[me],
+                feat_send.at[off - 1],
+                feat_recv.at[off - 1],
+                {"feat": peer},
+            )
+        )
+        last[-1].start()
+    fir_out[me] = fir_total[me]
+    finish(1, store_mixed)
+    for copy in last:
+        copy.wait()
+    for copy in list(pairs.values()) + list(sent.values()):
+        copy.wait_send()
+
+
+def reduce_stage(loaders, features, mixed, first):
+    chips = loaders // 2
+    dma = pltpu.SemaphoreType.DMA
+    vmem = pl.BlockSpec(memory_space=pltpu.VMEM)
+
+    def buffers(count):
+        return [pltpu.VMEM((count,) + a.shape[1:], jnp.bfloat16) for a in (mixed, first)]
+
+    return pl.pallas_call(
+        functools.partial(reduce_kernel, loaders, features),
+        in_specs=[vmem] * 2,
+        out_specs=[vmem] * 2,
+        out_shape=[
+            jax.ShapeDtypeStruct(mixed.shape[1:], jnp.float32),
+            jax.ShapeDtypeStruct(first.shape[1:], jnp.bfloat16),
+        ],
+        scratch_shapes=buffers(chips)
+        + buffers(chips)
+        + buffers(chips - 1)
+        + [
+            pltpu.VMEM(first.shape[1:], jnp.bfloat16),
+            dma((2, chips)),
+            dma((2, chips)),
+            dma((2, chips - 1)),
+            dma((2, chips - 1)),
+            dma((features - 1,)),
+            dma((features - 1,)),
+        ],
+        compiler_params=pltpu.CompilerParams(
+            collective_id=1, has_side_effects=True, vmem_limit_bytes=48 * 1024 * 1024
+        ),
+    )(mixed, first)
+
+
 def mixed_kernel(act_ref, tan_ref, grad_ref, fac_ref, fac_tan_ref, hess_ref, back_ref):
     rows = act_ref.shape[2]
     for b in range(act_ref.shape[0]):
@@ -283,29 +450,33 @@
         pre_tan_grad = (grad * (density * (2.0 - pre_act * pre_act)) * pre_tan).astype(
             jnp.bfloat16
         )
-        hess_ref[b] = lax.dot_general(
+        hess = lax.dot_general(
             jnp.concatenate([tan, act], axis=1),
             jnp.concatenate([pre_grad, pre_tan_grad], axis=1),
             (((1,), (1,)), ((), ())),
             preferred_element_type=jnp.float32,
-        ).astype(hess_ref.dtype)
+        )
+        parts, _, share, width = hess_ref.shape
+        hess_ref[:, b] = hess.reshape(parts, share, width).astype(hess_ref.dtype)
         back_ref[b] = (
             jnp.dot(fac, pre_tan_grad, preferred_element_type=jnp.float32)
             + jnp.dot(fac_tan, pre_grad, preferred_element_type=jnp.float32)
         ).astype(back_ref.dtype)
 
 
-def mixed_stage(act, tan, grad, fac, fac_tan):
+def mixed_stage(loaders, act, tan, grad, fac, fac_tan):
     blocks, width, rows = act.shape
     thin = pl.BlockSpec((STEP, width, rows), lambda s: (s, 0, 0))
     wide = pl.BlockSpec((STEP, width, width), lambda s: (s, 0, 0))
+    share = width // loaders
+    split = pl.BlockSpec((loaders, STEP, share, width), lambda s: (0, s, 0, 0))
     return pl.pallas_call(
         mixed_kernel,
         grid=(blocks // STEP,),
         in_specs=[thin, thin, thin, wide, wide],
-        out_specs=[wide, thin],
+        out_specs=[split, thin],
         out_shape=[
-            jax.ShapeDtypeStruct((blocks, width, width), jnp.bfloat16),
+            jax.ShapeDtypeStruct((loaders, blocks, share, width), jnp.bfloat16),
             jax.ShapeDtypeStruct((blocks, width, rows), jnp.bfloat16),
         ],
         compiler_params=pltpu.CompilerParams(vmem_limit_bytes=32 * 1024 * 1024),
@@ -393,8 +564,9 @@
     act = mix(first(factors[0], tok_all))
     tan = mix(first(factors[1], tok_all))
     grad = mix(first(factors[2], goal_all) * weight)
-    hess_mixed, back = mixed_stage(act, tan, grad, second_factor_blocks, second_factor_tangent)
-    hess_mixed = lax.psum_scatter(hess_mixed, "dp", scatter_dimension=1, tiled=True)
+    hess_mixed, back = mixed_stage(
+        loaders, act, tan, grad, second_factor_blocks, second_factor_tangent
+    )
 
     back = (
         back.reshape(local_blocks, all_blocks, pair, tok_count)
@@ -406,17 +578,16 @@
     hess_first = hess_first.astype(jnp.bfloat16).reshape(
         all_blocks, loaders, in_share * local_out
     )
-    hess_first = lax.psum_scatter(
-        hess_first.transpose(1, 0, 2), "dp", scatter_dimension=0, tiled=True
-    )
-    hess_first = hess_first.reshape(features, local_blocks, in_share * local_out)
-    hess_first = lax.all_to_all(hess_first, "feat", split_axis=0, concat_axis=0, tiled=True)
+    hess_first = hess_first.transpose(1, 0, 2).reshape(
+        loaders, features, local_blocks, in_share * local_out
+    )
+    hess_mixed, hess_first = reduce_stage(loaders, features, hess_mixed, hess_first)
     hess_first = (
         hess_first.reshape(features, local_blocks, in_share, local_out)
         .transpose(1, 2, 0, 3)
         .reshape(local_blocks, in_share, block_out)
     )
-    return hess_first.astype(jnp.float32), hess_mixed.astype(jnp.float32)
+    return hess_first.astype(jnp.float32), hess_mixed
 
 
 def solution(mesh):

time: 262 us -> 195 us (0.74)
  waiting for transfers between devices: 75.6 us -> 0 us
  Pallas kernels: 102 us -> 136 us
  between operations: 14.2 us -> 0.85 us
  blocking collectives: 10.5 us -> 0 us
    reduce_scatter x2 -> x0, waiting for transfers between devices: 74.9 us -> none  [the longest x1 41.7 us: per_device(): lax.psum_scatter(hess_mixed, 'dp', scatter_dimension=1, tiled=True)]
    pallas_call x0 -> x1, Pallas kernels: none -> 34.2 us  [reduce_stage(): pl.pallas_call(functools.partial(reduce_kernel, loaders, features), in_sp...]
    all_to_all x1 -> x0, blocking collectives: 10.5 us -> none  [per_device(): lax.all_to_all(hess_first, 'feat', split_axis=0, concat_axis=0, tiled=True)]
    unnamed x16 -> x17, local copies, waits for them, and re-layouts: 4.49 us -> 5.79 us
  transfers between devices with their start and end apart: 2 -> 0, of which waited for: 2 -> 0; matrix products, arithmetic and copies ran while one was open for 1% -> 0% of each run, Pallas kernels for 0% -> 0%
where the time goes in v3:
time: 195 us; the launch traced here: 194 us
  Pallas kernels  136 us (70%)
  local copies, waits for them, and re-layouts  41.8 us (21%)
  matrix products  13.2 us (7%)
  other arithmetic  2.21 us (1%)
    pallas_call x1, Pallas kernels, gather_stage(): pl.pallas_call(functools.partial(gather_kernel, loaders, features), in_sp...  87.3 us
    pallas_call x1, Pallas kernels, reduce_stage(): pl.pallas_call(functools.partial(reduce_kernel, loaders, features), in_sp...  34.2 us
    pallas_call x1, Pallas kernels, mixed_stage(): pl.pallas_call(mixed_kernel, grid=(blocks // STEP,), in_specs=[thin, thin...  14.5 us
    dot_general x3, matrix products, first(): jnp.einsum('jki,kir->kjr', weights, rows_of, preferred_element_type=jnp.f...  10.7 us
    reshape x3, local copies, waits for them, and re-layouts, mix(): return values.astype(jnp.bfloat16).reshape(all_blocks, local_blocks, pair...  9.28 us
    unnamed x17, local copies, waits for them, and re-layouts  5.79 us

profile of v3, /device:TPU:0, one launch (start us, length us, event | category | flops | bytes accessed | tf_op | source)
XLA Modules:
  0.0 194.1 jit_solution(13734003568311437701)
XLA Ops:
  0.6 0.9 select_reduce_fusion.1
  1.6 0.3 copy-done
  1.9 0.7 fusion.18
  2.6 0.2 reduce-window.4
  2.8 0.7 fusion.17
  3.8 0.1 fusion.11.send_sel_ref
  4.1 1.0 constant_dynamic-slice_fusion
  5.4 1.2 copy-done.6
  6.6 1.0 copy-done.7
  7.6 87.3 %shard_map.113 = (bf16[4,2048,128]{2,1,0:T(8,128)(2,1)S(1)}, bf16[4,2048,128]{2,1,0:T(8,128)(2,1)}, bf16[8,4,192,256]{3,2,1,0:T(8,128)(2,1)}) custom-call(bf16[128,2048]{1,0:T(8,128)(2,1)S(1)} %copy-done.7, bf16[256,2048]{1,0:T(8,128)(2,1)S(1)} %copy-done.6, bf16[256,256]{1,0:T(8,128)(2,1)S(1)} %fusion.11.send_sel_ref, ...), custom_call_target="tpu_custom_call" | custom-call | tf_op jit(solution)/shard_map/pallas_call | solution.py:232
  94.9 3.7 %copy.60 = bf16[8,4,3,64,256]{4,0,1,3,2:T(8,128)(2,1)S(1)} copy(bf16[8,4,3,64,256]{4,3,2,1,0:T(8,128)(2,1)} %bitcast.80) | data formatting | bytes 6291456 | tf_op jit(solution)/shard_map/reshape | solution.py:548
  98.5 1.8 fusion.19
  100.3 3.8 %squeeze.14 = bf16[64,128,64]{2,1,0:T(8,128)(2,1)} reshape(bf16[1,64,4,8,256]{4,3,2,1,0:T(8,128)(2,1)} %get-tuple-element.16) | data formatting | bytes 2097152 | tf_op jit(solution)/shard_map/squeeze | solution.py:566
  104.2 4.0 %multiply_convert_fusion = bf16[128,64,128]{2,1,0:T(8,128)(2,1)S(1)} fusion(bf16[128,64,128]{2,1,0:T(8,128)(2,1)} %bitcast.81, bf16[64,128,64]{2,1,0:T(8,128)(2,1)} %squeeze.14, f32[128]{0:T(128)S(1)} %divide_reduce_fusion), kind=kOutput, calls=%fused_computation | convolution fusion | flops 136314880 | bytes 5243392 | tf_op jit(solution)/shard_map/jki,kir->kjr/dot_general | solution.py:562
  108.1 3.6 %copy.44 = bf16[128,32,2,128]{3,2,0,1:T(2,128)(2,1)} copy(bf16[128,32,2,128]{3,2,1,0:T(2,128)(2,1)S(1)} %bitcast.75) | data formatting | bytes 4194304 | tf_op jit(solution)/shard_map/reshape | solution.py:556
  111.7 3.8 %squeeze.13 = bf16[64,128,64]{2,1,0:T(8,128)(2,1)} reshape(bf16[1,64,4,8,256]{4,3,2,1,0:T(8,128)(2,1)} %get-tuple-element.17) | data formatting | bytes 2097152 | tf_op jit(solution)/shard_map/squeeze | solution.py:565
  115.5 3.3 %fusion.8 = bf16[128,64,128]{2,1,0:T(8,128)(2,1)S(1)} fusion(bf16[128,64,128]{2,1,0:T(8,128)(2,1)S(1)} %bitcast.65, bf16[64,128,64]{2,1,0:T(8,128)(2,1)} %squeeze.13), kind=kOutput, calls=%fused_computation.8 | convolution fusion | flops 135266304 | bytes 5242880 | tf_op jit(solution)/shard_map/jki,kir->kjr/dot_general | solution.py:562
  118.8 3.5 %copy.42 = bf16[128,32,2,128]{3,2,0,1:T(2,128)(2,1)} copy(bf16[128,32,2,128]{3,2,1,0:T(2,128)(2,1)S(1)} %bitcast.77) | data formatting | bytes 4194304 | tf_op jit(solution)/shard_map/reshape | solution.py:556
  122.4 3.8 %squeeze.12 = bf16[64,128,64]{2,1,0:T(8,128)(2,1)} reshape(bf16[1,64,4,8,256]{4,3,2,1,0:T(8,128)(2,1)} %get-tuple-element.18) | data formatting | bytes 2097152 | tf_op jit(solution)/shard_map/squeeze | solution.py:564
  126.2 3.4 %fusion.5 = bf16[128,64,128]{2,1,0:T(8,128)(2,1)S(1)} fusion(bf16[128,64,128]{2,1,0:T(8,128)(2,1)S(1)} %bitcast.66, bf16[64,128,64]{2,1,0:T(8,128)(2,1)} %squeeze.12), kind=kOutput, calls=%fused_computation.7 | convolution fusion | flops 135266304 | bytes 5242880 | tf_op jit(solution)/shard_map/jki,kir->kjr/dot_general | solution.py:562
  129.6 2.2 %copy.40 = bf16[128,32,2,128]{3,2,0,1:T(2,128)(2,1)S(1)} copy(bf16[128,32,2,128]{3,2,1,0:T(2,128)(2,1)S(1)} %bitcast.78) | data formatting | bytes 4194304 | tf_op jit(solution)/shard_map/reshape | solution.py:556
  131.9 2.2 %copy-done.4 = bf16[32,256,256]{2,1,0:T(8,128)(2,1)S(1)} copy-done((bf16[32,256,256]{2,1,0:T(8,128)(2,1)S(1)}, bf16[32,256,256]{2,1,0:T(8,128)(2,1)}, u32[]{:S(2)}) %copy-start.4) | copy-done | bytes 4194328
  134.0 14.5 %shard_map.114 = (bf16[8,32,32,256]{3,2,1,0:T(8,128)(2,1)S(1)}, bf16[32,256,128]{2,1,0:T(8,128)(2,1)S(1)}) custom-call(bf16[32,256,128]{2,1,0:T(8,128)(2,1)S(1)} %bitcast.70, bf16[32,256,128]{2,1,0:T(8,128)(2,1)S(1)} %bitcast.69, bf16[32,256,128]{2,1,0:T(8,128)(2,1)S(1)} %bitcast.68, bf16[32,256,256]{2,1,0:T(8,128)(2,1)S(1)} %copy-done.3, ...), custom_call_target="tpu_custom_call" | custom-call | flops 3758096384 | bytes 20971520 | tf_op jit(solution)/shard_map/pallas_call | solution.py:473
  148.5 2.4 %copy.45 = bf16[128,32,2,128]{3,2,1,0:T(2,128)(2,1)S(1)} copy(bf16[128,32,2,128]{3,2,0,1:T(2,128)(2,1)S(1)} %bitcast.72) | data formatting | bytes 4194304 | tf_op jit(solution)/shard_map/transpose | solution.py:573
  150.9 2.6 %convolution_convert_fusion = bf16[128,64,64]{2,1,0:T(8,128)(2,1)} fusion(bf16[128,64,128]{2,1,0:T(8,128)(2,1)S(1)} %bitcast.67, bf16[128,64,128]{2,1,0:T(8,128)(2,1)S(1)} %bitcast.76), kind=kOutput, calls=%fused_computation.9 | convolution fusion | flops 134742016 | bytes 5242880 | tf_op jit(solution)/shard_map/kjr,kir->kij/dot_general | solution.py:576
  153.4 3.3 %copy.46 = bf16[128,64,64]{0,2,1:T(8,128)(2,1)S(1)} copy(bf16[128,64,64]{2,1,0:T(8,128)(2,1)} %convolution_convert_fusion) | data formatting | bytes 2097152 | tf_op jit(solution)/shard_map/convert_element_type | solution.py:578
  156.8 0.5 copy.47
  157.3 34.2 %shard_map.115 = (f32[32,32,256]{2,1,0:T(8,128)S(1)}, bf16[4,32,512]{2,1,0:T(8,128)(2,1)S(1)}) custom-call(bf16[8,32,32,256]{3,2,1,0:T(8,128)(2,1)} %copy-done.5, bf16[8,4,32,512]{3,2,1,0:T(8,128)(2,1)S(1)} %bitcast.71), custom_call_target="tpu_custom_call" | custom-call | tf_op jit(solution)/shard_map/pallas_call | solution.py:402
  191.6 0.1 reshape.125
  191.7 0.3 copy.48
  192.0 1.0 reshape.124
  193.1 1.0 copy.62
  (23 shorter events, 0.8 us)
Async XLA Ops:
  0.6 1.3 copy-start
  5.3 1.2 copy-start.6
  6.6 1.0 copy-start.7
  126.2 5.6 %copy-start.3 = (bf16[32,256,256]{2,1,0:T(8,128)(2,1)S(1)}, bf16[32,256,256]{2,1,0:T(8,128)(2,1)}, u32[]{:S(2)}) copy-start(bf16[32,256,256]{2,1,0:T(8,128)(2,1)} %fac_ref.1) | copy-start | bytes 12582916
  129.6 2.2 %copy-start.1 = (bf16[128,32,2,128]{3,2,0,1:T(2,128)(2,1)S(1)}, bf16[128,32,2,128]{3,2,0,1:T(2,128)(2,1)}, u32[]{:S(2)}) copy-start(bf16[128,32,2,128]{3,2,0,1:T(2,128)(2,1)} %copy.44) | copy-start | bytes 6291460
  129.6 2.2 %copy-start.2 = (bf16[128,32,2,128]{3,2,0,1:T(2,128)(2,1)S(1)}, bf16[128,32,2,128]{3,2,0,1:T(2,128)(2,1)}, u32[]{:S(2)}) copy-start(bf16[128,32,2,128]{3,2,0,1:T(2,128)(2,1)} %copy.42) | copy-start | bytes 6291460
  131.8 2.2 %copy-start.4 = (bf16[32,256,256]{2,1,0:T(8,128)(2,1)S(1)}, bf16[32,256,256]{2,1,0:T(8,128)(2,1)}, u32[]{:S(2)}) copy-start(bf16[32,256,256]{2,1,0:T(8,128)(2,1)} %fac_tan_ref.1) | copy-start | bytes 12582916
  148.5 2.4 %copy-start.5 = (bf16[8,32,32,256]{3,2,1,0:T(8,128)(2,1)}, bf16[8,32,32,256]{3,2,1,0:T(8,128)(2,1)S(1)}, u32[]{:S(2)}) copy-start(bf16[8,32,32,256]{3,2,1,0:T(8,128)(2,1)S(1)} %get-tuple-element.12.mix_ref) | copy-start | bytes 12582916

commit v4 on v3

--- a/solution.py
+++ b/solution.py
@@ -2,6 +2,7 @@
 
 import jax
 import jax.numpy as jnp
+import numpy as np
 from jax import lax
 from jax.experimental import pallas as pl
 from jax.experimental.pallas import tpu as pltpu
@@ -21,30 +22,15 @@
         body(pl.ds(pl.multiple_of(step * tile, tile), tile))
 
 
-def gather_kernel(
-    loaders,
-    features,
-    tok_ref,
-    target_ref,
-    send_sel_ref,
-    take_sel_ref,
-    fac_ref,
-    tok_all,
-    goal_all,
-    fac_all,
-    outgoing,
-    arrived,
-    slot_send,
-    slot_recv,
-    fac_send,
-    fac_recv,
-    chip_send,
-    chip_recv,
-    pair_send,
-    pair_recv,
-    line_send,
-    line_recv,
-):
+def gather_kernel(loaders, features, fused, *refs):
+    if fused:
+        spread_ref, keep_ref, weight_ref = refs[5:8]
+        act_out, tan_out, grad_out = refs[9:12]
+        refs = refs[:5] + (refs[8],) + refs[12:]
+    tok_ref, target_ref, send_sel_ref, take_sel_ref, fac_ref = refs[:5]
+    tok_all, goal_all, fac_all, outgoing, arrived = refs[5:10]
+    slot_send, slot_recv, fac_send, fac_recv, chip_send, chip_recv = refs[10:16]
+    pair_send, pair_recv, line_send, line_recv = refs[16:]
     dev = lax.axis_index("dp")
     me = lax.axis_index("feat")
     columns = tok_ref.shape[1]
@@ -207,38 +193,95 @@
 
     column_loop(columns, take)
     line_step(goal_all, 1, 0)
-    for step in range(2, features):
+    for step in range(2, features - 1):
         line_step(tok_all, 0, step)
     for off in range(1, chips):
         chip_copies[off - 1].wait_recv()
         piece = lax.rem(chip + chips - off, chips) * 2 + core
         pair_copies.append(to_pair(off, piece))
         pair_copies[-1].start()
-    for step in range(1, features):
-        line_step(goal_all, 1, step)
+    line_step(goal_all, 1, 1)
+    line_step(tok_all, 0, features - 1)
     for copy in pair_copies:
         copy.wait()
+
+    def first_stage(src, uses, lo, hi, near, far):
+        if not fused:
+            return
+        per_shard, pieces = fused
+        tall, wide = keep_ref.shape
+        width = tall // act_out.shape[0]
+        out_rows = spread_ref.shape[1]
+
+        @pl.loop(lo * per_shard, hi * per_shard)
+        def _(unit):
+            shard = unit // per_shard
+            part = unit % per_shard
+            distance = jnp.maximum(shard - me, me - shard)
+
+            @pl.when((distance >= near) & (distance <= far))
+            def _():
+                cols = src[shard, pl.ds(pl.multiple_of(part * wide, wide), wide), :]
+                for which, out in uses:
+                    rows = slice(which * out_rows, (which + 1) * out_rows)
+                    compact = jnp.concatenate(
+                        [fac_all[part * pieces + n, shard, rows, :] for n in range(pieces)], axis=1
+                    )
+                    spread = jnp.dot(
+                        spread_ref[...], compact, preferred_element_type=jnp.float32
+                    ).astype(jnp.bfloat16)
+                    value = jnp.dot(
+                        spread * keep_ref[...], cols, preferred_element_type=jnp.float32
+                    )
+                    if which == 2:
+                        value = value * weight_ref[...]
+                    place = pl.ds(pl.multiple_of(unit * width, width), width)
+                    out[:, place, :] = value.reshape(out.shape[0], width, out.shape[2]).astype(
+                        out.dtype
+                    )
+
+    if fused:
+        on_tok = ((0, act_out), (1, tan_out))
+        on_goal = ((2, grad_out),)
+    else:
+        on_tok = on_goal = ()
+    half = features // 2
+    first_stage(tok_all, on_tok, 0, half, 0, features)
+    for step in range(2, features - 1):
+        line_step(goal_all, 1, step)
+    first_stage(tok_all, on_tok, half, features, 0, features)
+    first_stage(goal_all, on_goal, 0, features, 0, features - 2)
+    line_step(goal_all, 1, features - 1)
+    first_stage(goal_all, on_goal, 0, features, features - 1, features)
     for copy in slot_copies + fac_copies + chip_copies:
         copy.wait_send()
     line_end(tok_all, 0)
     line_end(goal_all, 1)
 
 
-def gather_stage(loaders, features, tokens, targets, send_sel, take_sel, factors):
+def gather_stage(loaders, features, operands, fused):
+    tokens, _, send_sel, _, factors = operands[:5]
     rows, columns = tokens.shape
     slots = send_sel.shape[0]
     dma = pltpu.SemaphoreType.DMA
     vmem = pl.BlockSpec(memory_space=pltpu.VMEM)
+    shards = jax.ShapeDtypeStruct((features, columns, rows), jnp.bfloat16)
+    pieces = jax.ShapeDtypeStruct((loaders,) + factors.shape, jnp.bfloat16)
+    out_shape = [shards, shards, pieces]
+    held = []
+    if fused:
+        local_out = factors.shape[1] // 3
+        blocks = operands[5].shape[0] // 16
+        mixed = jax.ShapeDtypeStruct((blocks, features * local_out, rows), jnp.bfloat16)
+        held = [pltpu.VMEM(a.shape, a.dtype) for a in out_shape[1:]]
+        out_shape = [shards, mixed, mixed, mixed]
     return pl.pallas_call(
-        functools.partial(gather_kernel, loaders, features),
-        in_specs=[vmem] * 5,
-        out_specs=[vmem] * 3,
-        out_shape=[
-            jax.ShapeDtypeStruct((features, columns, rows), jnp.bfloat16),
-            jax.ShapeDtypeStruct((features, columns, rows), jnp.bfloat16),
-            jax.ShapeDtypeStruct((loaders,) + factors.shape, jnp.bfloat16),
-        ],
-        scratch_shapes=[
+        functools.partial(gather_kernel, loaders, features, fused),
+        in_specs=[vmem] * len(operands),
+        out_specs=[vmem] * len(out_shape),
+        out_shape=out_shape,
+        scratch_shapes=held
+        + [
             pltpu.VMEM((slots, columns), jnp.bfloat16),
             pltpu.VMEM((slots, columns), jnp.bfloat16),
             dma((loaders - 1,)),
@@ -255,7 +298,7 @@
         compiler_params=pltpu.CompilerParams(
             collective_id=0, has_side_effects=True, vmem_limit_bytes=48 * 1024 * 1024
         ),
-    )(tokens, targets, send_sel, take_sel, factors)
+    )(*operands)
 
 
 def reduce_kernel(
@@ -542,28 +585,44 @@
     )
     factors = factors.reshape(3, share, features, local_out).transpose(2, 0, 3, 1)
     factors = factors.reshape(features, 3 * local_out, share)
-    tok_all, goal_all, factors = gather_stage(
-        loaders, features, tokens, targets, send_sel, take_sel, factors
-    )
-    factors = factors.reshape(loaders, features, 3, local_out, share)
-    factors = factors.transpose(2, 3, 1, 0, 4).reshape(3, local_out, all_blocks, block_in)
-    tok_all = tok_all.reshape(all_blocks, block_in, tok_count)
-    goal_all = goal_all.reshape(all_blocks, block_in, tok_count)
-
-    def mix(values):
-        return (
-            values.astype(jnp.bfloat16)
-            .reshape(all_blocks, local_blocks, pair, tok_count)
-            .transpose(1, 0, 2, 3)
-            .reshape(local_blocks, block_out, tok_count)
-        )
-
-    def first(weights, rows_of):
-        return jnp.einsum("jki,kir->kjr", weights, rows_of, preferred_element_type=jnp.float32)
-
-    act = mix(first(factors[0], tok_all))
-    tan = mix(first(factors[1], tok_all))
-    grad = mix(first(factors[2], goal_all) * weight)
+    group = 16 // pair
+    wide = group * block_in
+    whole_pieces = share % block_in == 0 and wide % share == 0 and local_blocks % group == 0
+    fused = (local_blocks // group, wide // share) if whole_pieces else None
+    operands = (tokens, targets, send_sel, take_sel, factors)
+    if fused:
+        out_row = np.arange(16 * local_blocks)
+        column = (out_row // 16) * pair + out_row % pair
+        spread = column[:, None] == np.arange(local_out)[None, :]
+        keep = ((out_row % 16) // pair)[:, None] == (np.arange(wide) // block_in)[None, :]
+        operands += (
+            jnp.asarray(spread, jnp.bfloat16),
+            jnp.asarray(keep, jnp.bfloat16),
+            weight[None, :],
+        )
+        tok_all, act, tan, grad = gather_stage(loaders, features, operands, fused)
+        tok_all = tok_all.reshape(all_blocks, block_in, tok_count)
+    else:
+        tok_all, goal_all, factors = gather_stage(loaders, features, operands, None)
+        factors = factors.reshape(loaders, features, 3, local_out, share)
+        factors = factors.transpose(2, 3, 1, 0, 4).reshape(3, local_out, all_blocks, block_in)
+        tok_all = tok_all.reshape(all_blocks, block_in, tok_count)
+        goal_all = goal_all.reshape(all_blocks, block_in, tok_count)
+
+        def mix(values):
+            return (
+                values.astype(jnp.bfloat16)
+                .reshape(all_blocks, local_blocks, pair, tok_count)
+                .transpose(1, 0, 2, 3)
+                .reshape(local_blocks, block_out, tok_count)
+            )
+
+        def first(weights, rows_of):
+            return jnp.einsum("jki,kir->kjr", weights, rows_of, preferred_element_type=jnp.float32)
+
+        act = mix(first(factors[0], tok_all))
+        tan = mix(first(factors[1], tok_all))
+        grad = mix(first(factors[2], goal_all) * weight)
     hess_mixed, back = mixed_stage(
         loaders, act, tan, grad, second_factor_blocks, second_factor_tangent
     )

time: 195 us -> 174 us (0.89)
  local copies, waits for them, and re-layouts: 41.8 us -> 26.8 us
  matrix products: 13.2 us -> 1.22 us
  Pallas kernels: 136 us -> 141 us
    reshape x5 -> x1, local copies, waits for them, and re-layouts: 13.6 us -> 0.69 us  [the longest x3 9.28 us: mix(): return values.astype(jnp.bfloat16).reshape(all_blocks, local_blocks, pair...]
    squeeze x3 -> x0, local copies, waits for them, and re-layouts: 11.5 us -> none  [the longest x1 3.84 us: per_device(): grad = mix(first(factors[2], goal_all) * weight)]
    dot_general x3 -> x0, matrix products: 10.7 us -> none  [first(): jnp.einsum('jki,kir->kjr', weights, rows_of, preferred_element_type=jnp.f...]
    dynamic_slice x5, local copies, waits for them, and re-layouts: 1.31 us -> 7.34 us  [per_device(): lax.dynamic_slice_in_dim(w.reshape(rows, block_out), device * share, shar...]
    unnamed x17 -> x23, local copies, waits for them, and re-layouts: 5.79 us -> 10.4 us
    pallas_call x1, Pallas kernels: 87.3 us -> 91.1 us  [gather_stage(): pl.pallas_call(functools.partial(gather_kernel, loaders, features, fused)...]
where the time goes in v4:
time: 174 us; the launch traced here: 173 us
  Pallas kernels  141 us (81%)
  local copies, waits for them, and re-layouts  26.8 us (15%)
  other arithmetic  3.31 us (2%)
    pallas_call x1, Pallas kernels, gather_stage(): pl.pallas_call(functools.partial(gather_kernel, loaders, features, fused)...  91.1 us
    pallas_call x1, Pallas kernels, reduce_stage(): pl.pallas_call(functools.partial(reduce_kernel, loaders, features), in_sp...  35.5 us
    pallas_call x1, Pallas kernels, mixed_stage(): pl.pallas_call(mixed_kernel, grid=(blocks // STEP,), in_specs=[thin, thin...  14.6 us
    unnamed x23, local copies, waits for them, and re-layouts  10.4 us
    dynamic_slice x5, local copies, waits for them, and re-layouts, per_device(): lax.dynamic_slice_in_dim(w.reshape(rows, block_out), device * share, shar...  7.34 us

profile of v4, /device:TPU:0, one launch (start us, length us, event | category | flops | bytes accessed | tf_op | source)
XLA Modules:
  0.0 173.3 jit_solution(17889844544321941233)
XLA Ops:
  0.7 1.0 select_reduce_fusion.1
  1.7 0.2 copy-done
  1.9 0.7 fusion.7
  2.6 0.2 reduce-window.4
  2.8 0.7 fusion.6
  3.5 0.1 select_reduce_fusion
  3.6 0.1 divide_reduce_fusion
  3.7 0.1 iota_add_fusion
  3.7 0.1 add.43
  3.8 0.1 fusion.refs_2_
  3.9 0.7 constant_dynamic-slice_fusion.4
  4.6 1.7 copy.28
  6.3 1.7 constant_dynamic-slice_fusion
  8.0 1.7 copy.27
  9.6 1.7 copy.29
  11.3 1.1 pad_maximum_fusion
  12.4 91.1 %shard_map.131 = (bf16[4,2048,128]{2,1,0:T(8,128)(2,1)S(1)}, bf16[32,256,128]{2,1,0:T(8,128)(2,1)}, bf16[32,256,128]{2,1,0:T(8,128)(2,1)}, bf16[32,256,128]{2,1,0:T(8,128)(2,1)}) custom-call(bf16[128,2048]{1,0:T(8,128)(2,1)S(1)} %copy-done.8, bf16[256,2048]{1,0:T(8,128)(2,1)S(1)} %copy-done.7, bf16[256,256]{1,0:T(8,128)(2,1)S(1)} %fusion.refs_2_, ...), custom_call_target="tpu_custom_call" | custom-call | tf_op jit(solution)/shard_map/pallas_call | solution.py:278
  103.5 2.2 %copy-done.1 = bf16[32,256,256]{2,1,0:T(8,128)(2,1)S(1)} copy-done((bf16[32,256,256]{2,1,0:T(8,128)(2,1)S(1)}, bf16[32,256,256]{2,1,0:T(8,128)(2,1)}, u32[]{:S(2)}) %copy-start.1) | copy-done | bytes 4194328
  105.7 2.2 %copy-done.2 = bf16[32,256,256]{2,1,0:T(8,128)(2,1)S(1)} copy-done((bf16[32,256,256]{2,1,0:T(8,128)(2,1)S(1)}, bf16[32,256,256]{2,1,0:T(8,128)(2,1)}, u32[]{:S(2)}) %copy-start.2) | copy-done | bytes 4194328
  107.9 1.6 copy-done.4
  109.5 1.6 copy-done.5
  111.1 1.6 copy-done.6
  112.7 14.6 %shard_map.132 = (bf16[8,32,32,256]{3,2,1,0:T(8,128)(2,1)S(1)}, bf16[32,256,128]{2,1,0:T(8,128)(2,1)S(1)}) custom-call(bf16[32,256,128]{2,1,0:T(8,128)(2,1)S(1)} %copy-done.4, bf16[32,256,128]{2,1,0:T(8,128)(2,1)S(1)} %copy-done.5, bf16[32,256,128]{2,1,0:T(8,128)(2,1)S(1)} %copy-done.6, bf16[32,256,256]{2,1,0:T(8,128)(2,1)S(1)} %copy-done.1, ...), custom_call_target="tpu_custom_call" | custom-call | flops 3758096384 | bytes 20971520 | tf_op jit(solution)/shard_map/pallas_call | solution.py:516
  127.2 2.4 %copy.30 = bf16[128,32,2,128]{3,2,1,0:T(2,128)(2,1)S(1)} copy(bf16[128,32,2,128]{3,2,0,1:T(2,128)(2,1)S(1)} %bitcast.42) | data formatting | bytes 4194304 | tf_op jit(solution)/shard_map/transpose | solution.py:632
  129.6 1.2 convolution_convert_fusion
  130.9 2.9 %copy.31 = bf16[128,64,64]{0,2,1:T(8,128)(2,1)} copy(bf16[128,64,64]{2,1,0:T(8,128)(2,1)S(1)} %convolution_convert_fusion) | data formatting | bytes 2097152 | tf_op jit(solution)/shard_map/convert_element_type | solution.py:637
  133.8 1.5 copy.32
  135.3 35.5 %shard_map.133 = (f32[32,32,256]{2,1,0:T(8,128)S(1)}, bf16[4,32,512]{2,1,0:T(8,128)(2,1)S(1)}) custom-call(bf16[8,32,32,256]{3,2,1,0:T(8,128)(2,1)} %copy-done.3, bf16[8,4,32,512]{3,2,1,0:T(8,128)(2,1)S(1)} %bitcast.40), custom_call_target="tpu_custom_call" | custom-call | tf_op jit(solution)/shard_map/pallas_call | solution.py:445
  170.8 0.1 reshape.85
  170.9 0.3 copy.33
  171.2 1.0 reshape.84
  172.3 1.0 copy.35
  (18 shorter events, 0.1 us)
Async XLA Ops:
  0.6 1.3 copy-start
  0.6 11.7 %copy-start.9 = (bf16[512,512]{1,0:T(8,128)(2,1)S(1)}, bf16[512,512]{1,0:T(8,128)(2,1)}, u32[]{:S(2)}) copy-start(bf16[512,512]{1,0:T(8,128)(2,1)} %constant.33.clone.refs_6_) | copy-start | bytes 1572868
  0.7 11.7 %copy-start.10 = (bf16[512,64]{1,0:T(8,128)(2,1)S(1)}, bf16[512,64]{1,0:T(8,128)(2,1)}, u32[]{:S(2)}) copy-start(bf16[512,64]{1,0:T(8,128)(2,1)} %constant.32.clone.refs_5_) | copy-start | bytes 196612
  0.7 11.7 %copy-start.7 = (bf16[256,2048]{1,0:T(8,128)(2,1)S(1)}, bf16[256,2048]{1,0:T(8,128)(2,1)}, u32[]{:S(2)}) copy-start(bf16[256,2048]{1,0:T(8,128)(2,1)} %refs_1_.1) | copy-start | bytes 3145732
  0.7 11.7 %copy-start.8 = (bf16[128,2048]{1,0:T(8,128)(2,1)S(1)}, bf16[128,2048]{1,0:T(8,128)(2,1)}, u32[]{:S(2)}) copy-start(bf16[128,2048]{1,0:T(8,128)(2,1)} %refs_0_.1) | copy-start | bytes 1572868
  103.5 2.2 %copy-start.1 = (bf16[32,256,256]{2,1,0:T(8,128)(2,1)S(1)}, bf16[32,256,256]{2,1,0:T(8,128)(2,1)}, u32[]{:S(2)}) copy-start(bf16[32,256,256]{2,1,0:T(8,128)(2,1)} %fac_ref.1) | copy-start | bytes 12582916
  105.7 2.2 %copy-start.2 = (bf16[32,256,256]{2,1,0:T(8,128)(2,1)S(1)}, bf16[32,256,256]{2,1,0:T(8,128)(2,1)}, u32[]{:S(2)}) copy-start(bf16[32,256,256]{2,1,0:T(8,128)(2,1)} %fac_tan_ref.1) | copy-start | bytes 12582916
  107.9 1.6 copy-start.4
  109.5 1.6 copy-start.5
  111.1 1.6 copy-start.6
  127.2 2.4 %copy-start.3 = (bf16[8,32,32,256]{3,2,1,0:T(8,128)(2,1)}, bf16[8,32,32,256]{3,2,1,0:T(8,128)(2,1)S(1)}, u32[]{:S(2)}) copy-start(bf16[8,32,32,256]{3,2,1,0:T(8,128)(2,1)S(1)} %get-tuple-element.13.mix_ref) | copy-start | bytes 12582916

commit v5 on v4

--- a/solution.py
+++ b/solution.py
@@ -24,9 +24,14 @@
 
 def gather_kernel(loaders, features, fused, *refs):
     if fused:
-        spread_ref, keep_ref, weight_ref = refs[5:8]
-        act_out, tan_out, grad_out = refs[9:12]
-        refs = refs[:5] + (refs[8],) + refs[12:]
+        spread_ref, keep_ref, weight_ref = refs[4:7]
+        from_hbm = refs[7:12]
+        hess_out, back_out = refs[13:15]
+        act_out, tan_out, grad_out = refs[15:18]
+        share_refs = refs[18:21]
+        mix_fac, mix_fac_tan = refs[21:23]
+        local_sem = refs[23]
+        refs = refs[:4] + (refs[24], refs[12]) + refs[25:]
     tok_ref, target_ref, send_sel_ref, take_sel_ref, fac_ref = refs[:5]
     tok_all, goal_all, fac_all, outgoing, arrived = refs[5:10]
     slot_send, slot_recv, fac_send, fac_recv, chip_send, chip_recv = refs[10:16]
@@ -41,6 +46,24 @@
 
     def to_feat(peer):
         return {"feat": peer}
+
+    if fused:
+        share = share_refs[0].shape[0]
+        mine = pl.ds(pl.multiple_of(dev * share, share), share)
+        moves = [
+            pltpu.make_async_copy(src.at[mine] if n < 3 else src, dst, local_sem.at[n])
+            for n, (src, dst) in enumerate(zip(from_hbm, share_refs + (mix_fac, mix_fac_tan)))
+        ]
+        for move in moves:
+            move.start()
+        for n in range(3):
+            moves[n].wait()
+            turned = share_refs[n][...].T
+            out_rows = turned.shape[0] // features
+            for f in range(features):
+                fac_ref[f, n * out_rows : (n + 1) * out_rows] = turned[
+                    f * out_rows : (f + 1) * out_rows
+                ]
 
     barrier = pltpu.get_barrier_semaphore()
     for off in range(1, loaders):
@@ -253,6 +276,19 @@
     first_stage(goal_all, on_goal, 0, features, 0, features - 2)
     line_step(goal_all, 1, features - 1)
     first_stage(goal_all, on_goal, 0, features, features - 1, features)
+    if fused:
+        for move in moves[3:]:
+            move.wait()
+        parts, _, out_share, width = hess_out.shape
+
+        @pl.loop(0, act_out.shape[0])
+        def _(g):
+            hess, back = mixed_block(
+                act_out[g], tan_out[g], grad_out[g], mix_fac[g], mix_fac_tan[g]
+            )
+            hess_out[:, g] = hess.reshape(parts, out_share, width).astype(hess_out.dtype)
+            back_out[g] = back.astype(back_out.dtype)
+
     for copy in slot_copies + fac_copies + chip_copies:
         copy.wait_send()
     line_end(tok_all, 0)
@@ -260,24 +296,37 @@
 
 
 def gather_stage(loaders, features, operands, fused):
-    tokens, _, send_sel, _, factors = operands[:5]
+    tokens, _, send_sel, _ = operands[:4]
     rows, columns = tokens.shape
     slots = send_sel.shape[0]
     dma = pltpu.SemaphoreType.DMA
     vmem = pl.BlockSpec(memory_space=pltpu.VMEM)
+    in_specs = [vmem] * len(operands)
     shards = jax.ShapeDtypeStruct((features, columns, rows), jnp.bfloat16)
-    pieces = jax.ShapeDtypeStruct((loaders,) + factors.shape, jnp.bfloat16)
-    out_shape = [shards, shards, pieces]
     held = []
     if fused:
-        local_out = factors.shape[1] // 3
-        blocks = operands[5].shape[0] // 16
-        mixed = jax.ShapeDtypeStruct((blocks, features * local_out, rows), jnp.bfloat16)
-        held = [pltpu.VMEM(a.shape, a.dtype) for a in out_shape[1:]]
-        out_shape = [shards, mixed, mixed, mixed]
+        in_specs[7:] = [pl.BlockSpec(memory_space=pl.ANY)] * 5
+        in_rows, width = operands[7].shape
+        share = in_rows // loaders
+        blocks = operands[10].shape[0]
+        pieces = (features, 3 * width // features, share)
+        mixed = (blocks, width, rows)
+        out_shape = [
+            shards,
+            jax.ShapeDtypeStruct((loaders, blocks, width // loaders, width), jnp.bfloat16),
+            jax.ShapeDtypeStruct(mixed, jnp.bfloat16),
+        ]
+        shapes = [mixed] * 3 + [(share, width)] * 3 + [operands[10].shape] * 2
+        held = [pltpu.VMEM(shape, jnp.bfloat16) for shape in shapes]
+        held += [dma((5,))]
+        shapes = [pieces, shards.shape, (loaders,) + pieces]
+        held += [pltpu.VMEM(shape, jnp.bfloat16) for shape in shapes]
+    else:
+        pieces = jax.ShapeDtypeStruct((loaders,) + operands[4].shape, jnp.bfloat16)
+        out_shape = [shards, shards, pieces]
     return pl.pallas_call(
         functools.partial(gather_kernel, loaders, features, fused),
-        in_specs=[vmem] * len(operands),
+        in_specs=in_specs,
         out_specs=[vmem] * len(out_shape),
         out_shape=out_shape,
         scratch_shapes=held
@@ -468,43 +517,42 @@
     )(mixed, first)
 
 
+def mixed_block(act, tan, grad, fac, fac_tan):
+    rows = act.shape[1]
+    first_dims = (((0,), (0,)), ((), ()))
+    both = lax.dot_general(
+        fac,
+        jnp.concatenate([act, tan], axis=1),
+        first_dims,
+        preferred_element_type=jnp.float32,
+    )
+    pre_act = both[:, :rows]
+    pre_tan = both[:, rows:] + lax.dot_general(
+        fac_tan, act, first_dims, preferred_element_type=jnp.float32
+    )
+    grad = grad.astype(jnp.float32)
+    density = jnp.exp(-0.5 * pre_act * pre_act) * inv_root_two_pi
+    cdf = 0.5 * (1.0 + lax.erf(pre_act * inv_root_two))
+    pre_grad = (grad * (cdf + pre_act * density)).astype(jnp.bfloat16)
+    pre_tan_grad = (grad * (density * (2.0 - pre_act * pre_act)) * pre_tan).astype(jnp.bfloat16)
+    hess = lax.dot_general(
+        jnp.concatenate([tan, act], axis=1),
+        jnp.concatenate([pre_grad, pre_tan_grad], axis=1),
+        (((1,), (1,)), ((), ())),
+        preferred_element_type=jnp.float32,
+    )
+    back = jnp.dot(fac, pre_tan_grad, preferred_element_type=jnp.float32) + jnp.dot(
+        fac_tan, pre_grad, preferred_element_type=jnp.float32
+    )
+    return hess, back
+
+
 def mixed_kernel(act_ref, tan_ref, grad_ref, fac_ref, fac_tan_ref, hess_ref, back_ref):
-    rows = act_ref.shape[2]
+    parts, _, share, width = hess_ref.shape
     for b in range(act_ref.shape[0]):
-        act = act_ref[b]
-        tan = tan_ref[b]
-        fac = fac_ref[b]
-        fac_tan = fac_tan_ref[b]
-        first_dims = (((0,), (0,)), ((), ()))
-        both = lax.dot_general(
-            fac,
-            jnp.concatenate([act, tan], axis=1),
-            first_dims,
-            preferred_element_type=jnp.float32,
-        )
-        pre_act = both[:, :rows]
-        pre_tan = both[:, rows:] + lax.dot_general(
-            fac_tan, act, first_dims, preferred_element_type=jnp.float32
-        )
-        grad = grad_ref[b].astype(jnp.float32)
-        density = jnp.exp(-0.5 * pre_act * pre_act) * inv_root_two_pi
-        cdf = 0.5 * (1.0 + lax.erf(pre_act * inv_root_two))
-        pre_grad = (grad * (cdf + pre_act * density)).astype(jnp.bfloat16)
-        pre_tan_grad = (grad * (density * (2.0 - pre_act * pre_act)) * pre_tan).astype(
-            jnp.bfloat16
-        )
-        hess = lax.dot_general(
-            jnp.concatenate([tan, act], axis=1),
-            jnp.concatenate([pre_grad, pre_tan_grad], axis=1),
-            (((1,), (1,)), ((), ())),
-            preferred_element_type=jnp.float32,
-        )
-        parts, _, share, width = hess_ref.shape
+        hess, back = mixed_block(act_ref[b], tan_ref[b], grad_ref[b], fac_ref[b], fac_tan_ref[b])
         hess_ref[:, b] = hess.reshape(parts, share, width).astype(hess_ref.dtype)
-        back_ref[b] = (
-            jnp.dot(fac, pre_tan_grad, preferred_element_type=jnp.float32)
-            + jnp.dot(fac_tan, pre_grad, preferred_element_type=jnp.float32)
-        ).astype(back_ref.dtype)
+        back_ref[b] = back.astype(back_ref.dtype)
 
 
 def mixed_stage(loaders, act, tan, grad, fac, fac_tan):
@@ -577,19 +625,16 @@
 
     rows = local_blocks * block_in
     share = rows // loaders
-    factors = jnp.stack(
-        [
-            lax.dynamic_slice_in_dim(w.reshape(rows, block_out), device * share, share, 0)
-            for w in (first_blocks, first_tangent, jnp.swapaxes(down_blocks, 1, 2))
-        ]
-    )
-    factors = factors.reshape(3, share, features, local_out).transpose(2, 0, 3, 1)
-    factors = factors.reshape(features, 3 * local_out, share)
+    stacked = [
+        w.reshape(rows, block_out)
+        for w in (first_blocks, first_tangent, jnp.swapaxes(down_blocks, 1, 2))
+    ]
+
     group = 16 // pair
     wide = group * block_in
     whole_pieces = share % block_in == 0 and wide % share == 0 and local_blocks % group == 0
     fused = (local_blocks // group, wide // share) if whole_pieces else None
-    operands = (tokens, targets, send_sel, take_sel, factors)
+    operands = (tokens, targets, send_sel, take_sel)
     if fused:
         out_row = np.arange(16 * local_blocks)
         column = (out_row // 16) * pair + out_row % pair
@@ -599,11 +644,19 @@
             jnp.asarray(spread, jnp.bfloat16),
             jnp.asarray(keep, jnp.bfloat16),
             weight[None, :],
-        )
-        tok_all, act, tan, grad = gather_stage(loaders, features, operands, fused)
+            *stacked,
+            second_factor_blocks,
+            second_factor_tangent,
+        )
+        tok_all, hess_mixed, back = gather_stage(loaders, features, operands, fused)
         tok_all = tok_all.reshape(all_blocks, block_in, tok_count)
     else:
-        tok_all, goal_all, factors = gather_stage(loaders, features, operands, None)
+        factors = jnp.stack(
+            [lax.dynamic_slice_in_dim(w, device * share, share, 0) for w in stacked]
+        )
+        factors = factors.reshape(3, share, features, local_out).transpose(2, 0, 3, 1)
+        factors = factors.reshape(features, 3 * local_out, share)
+        tok_all, goal_all, factors = gather_stage(loaders, features, operands + (factors,), None)
         factors = factors.reshape(loaders, features, 3, local_out, share)
         factors = factors.transpose(2, 3, 1, 0, 4).reshape(3, local_out, all_blocks, block_in)
         tok_all = tok_all.reshape(all_blocks, block_in, tok_count)
@@ -623,9 +676,9 @@
         act = mix(first(factors[0], tok_all))
         tan = mix(first(factors[1], tok_all))
         grad = mix(first(factors[2], goal_all) * weight)
-    hess_mixed, back = mixed_stage(
-        loaders, act, tan, grad, second_factor_blocks, second_factor_tangent
-    )
+        hess_mixed, back = mixed_stage(
+            loaders, act, tan, grad, second_factor_blocks, second_factor_tangent
+        )
 
     back = (
         back.reshape(local_blocks, all_blocks, pair, tok_count)

time: 174 us -> 168 us (0.966)
  local copies, waits for them, and re-layouts: 26.8 us -> 18 us
  Pallas kernels: 141 us -> 145 us
    pallas_call x1, Pallas kernels: 91.1 us -> 110 us  [gather_stage(): pl.pallas_call(functools.partial(gather_kernel, loaders, features, fused)...]
    pallas_call x1 -> x0, Pallas kernels: 14.6 us -> none  [mixed_stage(): pl.pallas_call(mixed_kernel, grid=(blocks // STEP,), in_specs=[thin, thin...]
    dynamic_slice x5 -> x0, local copies, waits for them, and re-layouts: 7.34 us -> none  [per_device(): lax.dynamic_slice_in_dim(w.reshape(rows, block_out), device * share, shar...]
    unnamed x23 -> x17, local copies, waits for them, and re-layouts: 10.4 us -> 8.85 us
where the time goes in v5:
time: 168 us; the launch traced here: 167 us
  Pallas kernels  145 us (86%)
  local copies, waits for them, and re-layouts  18 us (11%)
  other arithmetic  2.08 us (1%)
    pallas_call x1, Pallas kernels, gather_stage(): pl.pallas_call(functools.partial(gather_kernel, loaders, features, fused)...  110 us
    pallas_call x1, Pallas kernels, reduce_stage(): pl.pallas_call(functools.partial(reduce_kernel, loaders, features), in_sp...  35.5 us
    unnamed x17, local copies, waits for them, and re-layouts  8.85 us
    transpose x1, local copies, waits for them, and re-layouts, per_device(): back = back.reshape(local_blocks, all_blocks, pair, tok_count).transpose(...  4.09 us

profile of v5, /device:TPU:0, one launch (start us, length us, event | category | flops | bytes accessed | tf_op | source)
XLA Modules:
  0.0 167.1 jit_solution(8826267758359271022)
XLA Ops:
  0.6 0.8 select_reduce_fusion.1
  1.5 0.7 fusion.4
  2.1 0.2 reduce-window.4
  2.3 0.7 fusion.3
  3.0 0.1 select_reduce_fusion
  3.1 0.1 divide_reduce_fusion
  3.2 0.1 iota_add_fusion
  3.3 0.1 add.38
  3.4 0.1 fusion.refs_2_
  3.5 0.0 copy-start
  3.5 1.2 copy-done
  4.7 0.0 copy-start.1
  4.7 1.2 copy-done.1
  6.0 0.0 copy-start.2
  6.0 1.2 copy-done.2
  7.2 0.0 copy-start.3
  7.2 1.2 copy-done.3
  8.4 1.0 copy-done.4
  9.5 1.0 copy-done.5
  10.5 0.9 copy-done.6
  11.4 109.6 %shard_map.131 = (bf16[4,2048,128]{2,1,0:T(8,128)(2,1)}, bf16[8,32,32,256]{3,2,1,0:T(8,128)(2,1)}, bf16[32,256,128]{2,1,0:T(8,128)(2,1)}) custom-call(bf16[128,2048]{1,0:T(8,128)(2,1)S(1)} %copy-done.4, bf16[256,2048]{1,0:T(8,128)(2,1)S(1)} %copy-done, bf16[256,256]{1,0:T(8,128)(2,1)S(1)} %fusion.refs_2_, bf16[256,128]{1,0:T(8,128)(2,1)S(1)} %fusion.1.refs_3_, ...), custom_call_target="tpu_custom_call" | custom-call | tf_op jit(solution)/shard_map/pallas_call | solution.py:327
  121.0 0.0 copy-start.7
  121.0 4.1 %copy.21 = bf16[128,32,2,128]{3,2,1,0:T(2,128)(2,1)S(1)} copy(bf16[128,32,2,128]{3,2,0,1:T(2,128)(2,1)} %bitcast.42) | data formatting | bytes 4194304 | tf_op jit(solution)/shard_map/transpose | solution.py:685
  125.1 0.0 copy-done.7
  125.1 1.2 convolution_convert_fusion
  126.4 2.2 %copy.22 = bf16[128,64,64]{0,2,1:T(8,128)(2,1)S(1)} copy(bf16[128,64,64]{2,1,0:T(8,128)(2,1)S(1)} %convolution_convert_fusion) | data formatting | bytes 2097152 | tf_op jit(solution)/shard_map/convert_element_type | solution.py:690
  128.6 0.5 copy.23
  129.1 35.5 %shard_map.132 = (f32[32,32,256]{2,1,0:T(8,128)S(1)}, bf16[4,32,512]{2,1,0:T(8,128)(2,1)S(1)}) custom-call(bf16[8,32,32,256]{3,2,1,0:T(8,128)(2,1)} %get-tuple-element.7.mix_ref, bf16[8,4,32,512]{3,2,1,0:T(8,128)(2,1)S(1)} %bitcast.33), custom_call_target="tpu_custom_call" | custom-call | tf_op jit(solution)/shard_map/pallas_call | solution.py:494
  164.6 0.1 reshape.74
  164.7 0.3 copy.24
  165.1 1.0 reshape.73
  166.1 1.0 copy.26
  (5 shorter events, 0.0 us)
Async XLA Ops:
  3.5 1.2 copy-start
  4.7 1.2 copy-start.1
  6.0 1.2 copy-start.2
  7.2 1.2 copy-start.3
  8.4 1.0 copy-start.4
  9.5 1.0 copy-start.5
  10.5 0.9 copy-start.6
  121.0 4.1 %copy-start.7 = (bf16[4,2048,128]{2,1,0:T(8,128)(2,1)S(1)}, bf16[4,2048,128]{2,1,0:T(8,128)(2,1)}, u32[]{:S(2)}) copy-start(bf16[4,2048,128]{2,1,0:T(8,128)(2,1)} %get-tuple-element.8) | copy-start | bytes 6291460

commit v6 on v5

--- a/solution.py
+++ b/solution.py
@@ -345,7 +345,7 @@
             dma((2, 2, features - 1)),
         ],
         compiler_params=pltpu.CompilerParams(
-            collective_id=0, has_side_effects=True, vmem_limit_bytes=48 * 1024 * 1024
+            collective_id=0, has_side_effects=True, vmem_limit_bytes=60 * 1024 * 1024
         ),
     )(*operands)
 

time: 168 us -> 163 us (0.970)
  local copies, waits for them, and re-layouts: 18 us -> 10.1 us
  Pallas kernels: 145 us -> 147 us
  other arithmetic: 2.08 us -> 3.85 us
    unnamed x17 -> x3, local copies, waits for them, and re-layouts: 8.85 us -> 0.97 us
    pallas_call x1, Pallas kernels: 110 us -> 112 us  [gather_stage(): pl.pallas_call(functools.partial(gather_kernel, loaders, features, fused)...]
where the time goes in v6:
time: 163 us
  Pallas kernels  147 us (90%)
  local copies, waits for them, and re-layouts  10.1 us (6%)
  other arithmetic  3.85 us (2%)
    pallas_call x1, Pallas kernels, gather_stage(): pl.pallas_call(functools.partial(gather_kernel, loaders, features, fused)...  112 us
    pallas_call x1, Pallas kernels, reduce_stage(): pl.pallas_call(functools.partial(reduce_kernel, loaders, features), in_sp...  35.5 us
    transpose x1, local copies, waits for them, and re-layouts, per_device(): back = back.reshape(local_blocks, all_blocks, pair, tok_count).transpose(...  4.09 us

profile of v6, /device:TPU:0, one launch (start us, length us, event | category | flops | bytes accessed | tf_op | source)
XLA Modules:
  0.0 163.0 jit_solution(13006701058395924279)
XLA Ops:
  0.6 0.8 select_reduce_fusion.1
  1.5 0.7 fusion.4
  2.1 0.2 reduce-window.4
  2.3 0.7 fusion.3
  3.0 0.1 select_reduce_fusion
  3.1 0.6 divide_reduce_fusion
  3.7 0.1 iota_add_fusion
  3.8 0.1 add.38
  3.9 0.7 fusion.1.refs_3_
  4.5 0.8 fusion.refs_2_
  5.3 111.6 %shard_map.131 = (bf16[4,2048,128]{2,1,0:T(8,128)(2,1)}, bf16[8,32,32,256]{3,2,1,0:T(8,128)(2,1)}, bf16[32,256,128]{2,1,0:T(8,128)(2,1)}) custom-call(bf16[128,2048]{1,0:T(8,128)(2,1)} %refs_0_.1, bf16[256,2048]{1,0:T(8,128)(2,1)} %refs_1_.1, bf16[256,256]{1,0:T(8,128)(2,1)} %fusion.refs_2_, bf16[256,128]{1,0:T(8,128)(2,1)} %fusion.1.refs_3_, ...), custom_call_target="tpu_custom_call" | custom-call | tf_op jit(solution)/shard_map/pallas_call | solution.py:327
  116.9 0.0 copy-start
  116.9 4.1 %copy.21 = bf16[128,32,2,128]{3,2,1,0:T(2,128)(2,1)S(1)} copy(bf16[128,32,2,128]{3,2,0,1:T(2,128)(2,1)} %bitcast.38) | data formatting | bytes 4194304 | tf_op jit(solution)/shard_map/transpose | solution.py:685
  121.0 0.0 copy-done
  121.0 1.2 convolution_convert_fusion
  122.2 2.2 %copy.22 = bf16[128,64,64]{0,2,1:T(8,128)(2,1)S(1)} copy(bf16[128,64,64]{2,1,0:T(8,128)(2,1)S(1)} %convolution_convert_fusion) | data formatting | bytes 2097152 | tf_op jit(solution)/shard_map/convert_element_type | solution.py:690
  124.5 0.5 copy.23
  125.0 35.5 %shard_map.132 = (f32[32,32,256]{2,1,0:T(8,128)S(1)}, bf16[4,32,512]{2,1,0:T(8,128)(2,1)S(1)}) custom-call(bf16[8,32,32,256]{3,2,1,0:T(8,128)(2,1)} %get-tuple-element.7.mix_ref, bf16[8,4,32,512]{3,2,1,0:T(8,128)(2,1)S(1)} %bitcast.33), custom_call_target="tpu_custom_call" | custom-call | tf_op jit(solution)/shard_map/pallas_call | solution.py:494
  160.5 0.1 reshape.74
  160.6 0.3 copy.24
  161.0 1.0 reshape.73
  162.0 1.0 copy.26
  (1 shorter events, 0.0 us)
Async XLA Ops:
  116.9 4.1 %copy-start = (bf16[4,2048,128]{2,1,0:T(8,128)(2,1)S(1)}, bf16[4,2048,128]{2,1,0:T(8,128)(2,1)}, u32[]{:S(2)}) copy-start(bf16[4,2048,128]{2,1,0:T(8,128)(2,1)} %get-tuple-element.8) | copy-start | bytes 6291460
